TPU v7x, 32 devices: a whole 2x2x4 slice. The times are simulated.
32 devices in a mesh: groups: 2 (over y), feat: 16 (over z, x, core).
Axes of the slice: x: 2, y: 2, z: 4, core: 2. Of those that a mesh axis runs over, the one named last changes fastest.
Arguments:
- node_features: bfloat16 [768, 16384], P('feat', 'groups'), parts along dimension 1, may hold values from -6 to 6
- neighbors_one: int32 [4096, 25], P('groups'), parts along dimension 0, may hold values from 0 to 8191
- weight_self_one: bfloat16 [768, 1024], replicated, may hold values from -0.21875 to 0.21875
- weight_neigh_one: bfloat16 [768, 1024], replicated, may hold values from -0.21875 to 0.21875
- bias_one: bfloat16 [1024], replicated, may hold values from -3 to 3
- weight_self_two: bfloat16 [1024, 1024], replicated, may hold values from -0.1875 to 0.1875
- weight_neigh_two: bfloat16 [1024, 1024], replicated, may hold values from -0.1875 to 0.1875
- send_rows: int32 [16, 16, 4], P('feat', None, 'groups'), parts along dimension 2, may hold values from 0 to 127
- neighbors_two: int32 [2048, 15], P(('groups', 'feat')), parts along dimension 0, may hold values from 0 to 31
- degree_two: int32 [2048], P(('groups', 'feat')), parts along dimension 0, may hold values from 1 to 15
- out_grad: bfloat16 [2048, 1024], P(('groups', 'feat')), parts along dimension 0, may hold values from -0.1875 to 0.1875
Outputs:
- layer_out: bfloat16 [2048, 1024], P(('groups', 'feat')), parts along dimension 0
- grad_self_one: float32 [768, 2048], P('feat', 'groups'), parts along dimension 1
- grad_neigh_one: float32 [768, 2048], P('feat', 'groups'), parts along dimension 1
- grad_self_two: float32 [1024, 2048], P('feat', 'groups'), parts along dimension 1
- grad_neigh_two: float32 [1024, 2048], P('feat', 'groups'), parts along dimension 1
There are 2 independent parts, one for each index of `groups`. A program takes and returns all parts, laid end to end along the dimension named above; an argument that names none is the same for every part. Nothing has to cross between parts.
Inputs may be any that keep to these rules, and one draw needn't show every extreme that they name: `neighbors_one`: sampled neighbors may repeat. send_rows[s, b, c] is one of the 128 layer-one rows owned by block s, provided in slot c to block b; a row may fill several slots. `neighbors_two`: entries at positions k >= degree_two[j] are ignored.
All inputs are finite; a program needn't handle non-finite values.
Results may differ from a plain program's by a relative error of at most 0.0052.
Values may be sent and summed in bfloat16 or wider, within the bound.
A program may use at most 320 MiB of HBM per device.

v0:
```python
import jax
import jax.numpy as jnp
from jax import lax
from jax.sharding import PartitionSpec as P


def gelu_tanh(argument):
    return jax.nn.gelu(argument, approximate=True)


def contract_lead(left_side, right_side):
    return lax.dot_general(
        left_side, right_side, (((0,), (0,)), ((), ())), preferred_element_type=jnp.float32
    )


def contract_last(left_side, right_side):
    return lax.dot_general(
        left_side, right_side, (((1,), (1,)), ((), ())), preferred_element_type=jnp.float32
    )


def exact_lead(left_side, right_side):
    return lax.dot_general(
        left_side,
        right_side,
        (((0,), (0,)), ((), ())),
        precision=lax.Precision.HIGHEST,
        preferred_element_type=jnp.float32,
    )


def shards(
    node_features,
    neighbors_one,
    weight_self_one,
    weight_neigh_one,
    bias_one,
    weight_self_two,
    weight_neigh_two,
    send_rows,
    neighbors_two,
    degree_two,
    out_grad,
):
    devices = lax.axis_size("feat")
    hidden_width = weight_self_two.shape[0]
    own_seeds = out_grad.shape[0]
    targets = neighbors_one.shape[0]
    own_rows = targets // devices
    fanout_one = neighbors_one.shape[1]
    block_rows = jnp.arange(targets, dtype=jnp.int32).reshape(devices, 1, own_rows)
    fan_major = jnp.transpose(neighbors_one.reshape(devices, own_rows, fanout_one), (0, 2, 1))
    wanted = jnp.concatenate([block_rows, fan_major], axis=1)
    picked = jnp.take(node_features, wanted.reshape(devices, -1), axis=1)
    arrived = lax.all_to_all(picked, "feat", split_axis=1, concat_axis=0, tiled=True)
    full_width = arrived.shape[0]
    arrived = arrived.reshape(full_width, fanout_one + 1, own_rows)
    self_cols = arrived[:, 0, :]
    mean_cols = (jnp.sum(arrived[:, 1:, :].astype(jnp.float32), axis=1) / fanout_one).astype(
        jnp.bfloat16
    )
    pre_one = (
        contract_lead(self_cols, weight_self_one)
        + contract_lead(mean_cols, weight_neigh_one)
        + bias_one.astype(jnp.float32)
    )
    hidden_one = gelu_tanh(pre_one).astype(jnp.bfloat16)
    peer_rows = send_rows[0]
    slots_peer = peer_rows.shape[1]
    slot_total = devices * slots_peer
    outgoing = jnp.take(hidden_one, peer_rows.reshape(-1), axis=0).reshape(
        devices, slots_peer, hidden_width
    )
    incoming = lax.all_to_all(outgoing, "feat", split_axis=0, concat_axis=0, tiled=True)
    fanout_two = neighbors_two.shape[1]
    keep_mask = jnp.arange(fanout_two, dtype=jnp.int32)[None, :] < degree_two[:, None]
    slot_ids = jnp.arange(slot_total, dtype=jnp.int32)
    slot_hits = (neighbors_two[:, :, None] == slot_ids[None, None, :]) & keep_mask[:, :, None]
    ref_count = jnp.sum(slot_hits.astype(jnp.float32), axis=1)
    degree_float = degree_two.astype(jnp.float32)[:, None]
    summed_two = jnp.dot(
        ref_count.astype(jnp.bfloat16),
        incoming.reshape(slot_total, hidden_width),
        preferred_element_type=jnp.float32,
    )
    mean_two = (summed_two / degree_float).astype(jnp.bfloat16)
    seed_hidden = hidden_one[:own_seeds]
    out_full = jnp.dot(seed_hidden, weight_self_two, preferred_element_type=jnp.float32) + jnp.dot(
        mean_two, weight_neigh_two, preferred_element_type=jnp.float32
    )
    layer_out = out_full.astype(jnp.bfloat16)
    back_self = contract_last(out_grad, weight_self_two)
    per_neighbor = contract_last(out_grad, weight_neigh_two) / degree_float
    slot_grads = exact_lead(ref_count, per_neighbor)
    returned = lax.all_to_all(
        slot_grads.reshape(devices, slots_peer, hidden_width),
        "feat",
        split_axis=0,
        concat_axis=0,
        tiled=True,
    )
    row_hits = (
        peer_rows.reshape(-1)[:, None] == jnp.arange(own_rows, dtype=jnp.int32)[None, :]
    ).astype(jnp.float32)
    grad_hidden = exact_lead(row_hits, returned.reshape(slot_total, hidden_width))
    grad_hidden = grad_hidden + jnp.pad(back_self, ((0, own_rows - own_seeds), (0, 0)))
    _, pull_back = jax.vjp(gelu_tanh, pre_one)
    grad_pre = pull_back(grad_hidden)[0].astype(jnp.bfloat16)
    own_part = self_cols
    mean_part = mean_cols
    both_one = lax.psum_scatter(
        jnp.concatenate(
            [
                jnp.dot(own_part, grad_pre, preferred_element_type=jnp.float32),
                jnp.dot(mean_part, grad_pre, preferred_element_type=jnp.float32),
            ],
            axis=1,
        ),
        "feat",
        scatter_dimension=0,
        tiled=True,
    )
    grad_self_one = both_one[:, :hidden_width]
    grad_neigh_one = both_one[:, hidden_width:]
    own_part = seed_hidden
    mean_part = mean_two
    both_two = lax.psum_scatter(
        jnp.concatenate(
            [contract_lead(own_part, out_grad), contract_lead(mean_part, out_grad)], axis=1
        ),
        "feat",
        scatter_dimension=0,
        tiled=True,
    )
    return (
        layer_out,
        grad_self_one,
        grad_neigh_one,
        both_two[:, :hidden_width],
        both_two[:, hidden_width:],
    )


def solution(mesh):
    return jax.shard_map(
        shards,
        mesh=mesh,
        in_specs=(
            P("feat", "groups"),
            P("groups", None),
            P(),
            P(),
            P(),
            P(),
            P(),
            P("feat", None, "groups"),
            P(("groups", "feat"), None),
            P(("groups", "feat")),
            P(("groups", "feat"), None),
        ),
        out_specs=(
            P(("groups", "feat"), None),
            P("feat", "groups"),
            P("feat", "groups"),
            P("feat", "groups"),
            P("feat", "groups"),
        ),
        check_vma=False,
    )
```

profile of v0, /device:TPU:1, one launch (start us, length us, event | category | flops | bytes accessed | tf_op | source)
XLA Modules:
  0.0 568.2 jit_solution(5157758904434112851)
XLA Ops:
  7.2 0.8 convert_element_type.39
  8.0 0.7 iota_compare_fusion.3
  8.7 0.8 convert_reduce_fusion.1
  9.4 2.4 fusion.1
  12.1 0.8 copy.52
  12.9 7.3 %all-to-all-start.2 = ((f32[16,2,1024]{2,1,0:T(2,128)}), f32[16,2,1024]{2,1,0:T(2,128)S(1)}, u32[]{:S(2)}, u32[]{:S(2)}) async-start(f32[16,2,1024]{2,1,0:T(2,128)} %copy.52), calls=%async_computation.2 | async-start | bytes 262144 | tf_op jit(solution)/shard_map/all_to_all | solution.py:96
  20.6 2.7 copy.46
  23.3 178.9 %gather_fusion = bf16[53248,48]{1,0:T(8,128)(2,1)} fusion(bf16[48,8192]{0,1:T(8,128)(2,1)} %copy.46, s32[53248]{0:T(1024)S(1)} %broadcast_clamp_fusion), kind=kCustom, calls=%fused_computation | custom fusion | bytes 10436608 | tf_op jit(solution)/shard_map/jit(_take)/gather | solution.py:55
  202.2 13.0 %copy.47 = bf16[16,3328,48]{1,2,0:T(8,128)(2,1)} copy(bf16[16,3328,48]{2,1,0:T(8,128)(2,1)} %bitcast.58) | data formatting | bytes 10223616 | tf_op jit(solution)/shard_map/jit(_take)/gather | solution.py:55
  215.4 5.3 select_bitcast_fusion
  220.6 6.2 %all-to-all-start = ((bf16[48,16,3328]{2,0,1:T(8,128)(2,1)}), bf16[48,16,3328]{2,0,1:T(8,128)(2,1)}, u32[]{:S(2)}, u32[]{:S(2)}) async-start(bf16[48,16,3328]{2,0,1:T(8,128)(2,1)} %select_bitcast_fusion), calls=%async_computation | async-start | bytes 10223616 | tf_op jit(solution)/shard_map/all_to_all | solution.py:56
  227.3 0.8 fusion.32
  228.1 92.8 %all-to-all-done = bf16[48,16,3328]{2,0,1:T(8,128)(2,1)} async-done(((bf16[48,16,3328]{2,0,1:T(8,128)(2,1)}), bf16[48,16,3328]{2,0,1:T(8,128)(2,1)}, u32[]{:S(2)}, u32[]{:S(2)}) %all-to-all-start) | async-done | bytes 5111840 | tf_op jit(solution)/shard_map/all_to_all | solution.py:56
  320.9 9.7 %reshape.162 = bf16[768,26,128]{2,1,0:T(8,128)(2,1)} reshape(bf16[16,48,1,3328]{3,1,0,2:T(8,128)(2,1)} %bitcast.4) | data formatting | bytes 10223616 | tf_op jit(solution)/shard_map/reshape | solution.py:58
  330.6 1.6 slice.32
  332.2 9.6 %convert_reduce_fusion = f32[768,128]{1,0:T(8,128)S(1)} fusion(bf16[768,26,128]{2,1,0:T(8,128)(2,1)} %reshape.162), kind=kLoop, calls=%fused_computation.2 | loop fusion | flops 4816896 | bytes 5308416 | tf_op jit(solution)/shard_map/reduce_sum | solution.py:60
  342.9 0.8 fusion.10
  344.8 3.1 pad_maximum_fusion.1
  348.1 0.6 gather_fusion.1
  348.7 0.8 broadcast_select_fusion
  349.5 23.0 %all-to-all-start.1 = ((bf16[16,2,1024]{2,1,0:T(2,128)(2,1)}), bf16[16,2,1024]{2,1,0:T(2,128)(2,1)S(1)}, u32[]{:S(2)}, u32[]{:S(2)}) async-start(bf16[16,2,1024]{2,1,0:T(2,128)(2,1)} %broadcast_select_fusion), calls=%async_computation.1 | async-start | bytes 131072 | tf_op jit(solution)/shard_map/all_to_all | solution.py:75
  372.7 2.7 fusion.16
  375.4 3.1 all-to-all-done.1
  378.8 0.8 fusion.33
  379.5 1.5 copy-done.1
  381.1 4.3 pad_maximum_fusion
  385.4 9.3 %copy.55 = f32[1024,2048]{1,0:T(8,128)} copy(f32[1024,2048]{0,1:T(8,128)} %pad_maximum_fusion) | data formatting | bytes 16777216
  395.2 2.8 fusion.2
  398.0 52.2 %reduce-scatter.5.cloned.1.call-done = f32[48,2048]{1,0:T(8,128)} async-done(((f32[768,2048]{1,0:T(8,128)}), f32[48,2048]{1,0:T(8,128)}) %reduce-scatter.5.cloned.1.call-update) | async-done | bytes 393232 | tf_op jit(solution)/shard_map/reduce_scatter | solution.py:112
  450.3 1.8 fusion.31
  452.1 107.4 %reduce-scatter.7.cloned.1.call-done = f32[64,2048]{1,0:T(8,128)} async-done(((f32[1024,2048]{1,0:T(8,128)}), f32[64,2048]{1,0:T(8,128)}) %reduce-scatter.7.cloned.1.call-update) | async-done | bytes 524304
  559.5 1.9 fusion.30
  (48 shorter events, 4.6 us)
Async XLA Ops:
  7.2 220.1 %copy-start = (bf16[1024,1024]{1,0:T(8,128)(2,1)S(1)}, bf16[1024,1024]{1,0:T(8,128)(2,1)}, u32[]{:S(2)}) copy-start(bf16[1024,1024]{1,0:T(8,128)(2,1)} %param.16) | copy-start | bytes 6291460
  7.2 13.0 %copy-start.5 = (s32[2048,25]{0,1:T(8,128)S(1)}, s32[2048,25]{0,1:T(8,128)}, u32[]{:S(2)}) copy-start(s32[2048,25]{0,1:T(8,128)} %param.12) | copy-start | bytes 614404
  12.9 207.7 %all-to-all-start.2 = ((f32[16,2,1024]{2,1,0:T(2,128)}), f32[16,2,1024]{2,1,0:T(2,128)S(1)}, u32[]{:S(2)}, u32[]{:S(2)}) async-start(f32[16,2,1024]{2,1,0:T(2,128)} %copy.52), calls=%async_computation.2 | async-start | bytes 262144 | tf_op jit(solution)/shard_map/all_to_all | solution.py:96
  220.6 6.4 %copy-start.6 = (bf16[1024]{0:T(1024)(128)(2,1)S(1)}, bf16[1024]{0:T(1024)(128)(2,1)}, u32[]{:S(2)}) copy-start(bf16[1024]{0:T(1024)(128)(2,1)} %param.15) | copy-start | bytes 6148
  220.6 6.4 %copy-start.7 = (s32[1,16,2]{1,2,0:T(2,128)S(1)}, s32[1,16,2]{1,2,0:T(2,128)}, u32[]{:S(2)}) copy-start(s32[1,16,2]{1,2,0:T(2,128)} %param.18) | copy-start | bytes 388
  220.6 6.6 %copy-start.2 = (bf16[64,1024]{1,0:T(8,128)(2,1)S(1)}, bf16[64,1024]{1,0:T(8,128)(2,1)}, u32[]{:S(2)}) copy-start(bf16[64,1024]{1,0:T(8,128)(2,1)} %param.21) | copy-start | bytes 393220
  220.6 100.2 %all-to-all-start = ((bf16[48,16,3328]{2,0,1:T(8,128)(2,1)}), bf16[48,16,3328]{2,0,1:T(8,128)(2,1)}, u32[]{:S(2)}, u32[]{:S(2)}) async-start(bf16[48,16,3328]{2,0,1:T(8,128)(2,1)} %select_bitcast_fusion), calls=%async_computation | async-start | bytes 10223616 | tf_op jit(solution)/shard_map/all_to_all | solution.py:56
  226.8 223.5 %reduce-scatter.5.cloned.1.call-start = ((), (), s32[]{:S(2)}) async-start(), calls=%async_computation.5 | async-start | bytes 6684672 | tf_op jit(solution)/shard_map/reduce_scatter | solution.py:112
  332.2 9.7 %copy-start.3 = (bf16[768,1024]{1,0:T(8,128)(2,1)S(1)}, bf16[768,1024]{1,0:T(8,128)(2,1)}, u32[]{:S(2)}) copy-start(bf16[768,1024]{1,0:T(8,128)(2,1)} %param.13) | copy-start | bytes 4718596
  332.2 10.1 %copy-start.4 = (bf16[768,1024]{1,0:T(8,128)(2,1)S(1)}, bf16[768,1024]{1,0:T(8,128)(2,1)}, u32[]{:S(2)}) copy-start(bf16[768,1024]{1,0:T(8,128)(2,1)} %param.14) | copy-start | bytes 4718596
  349.5 29.0 %all-to-all-start.1 = ((bf16[16,2,1024]{2,1,0:T(2,128)(2,1)}), bf16[16,2,1024]{2,1,0:T(2,128)(2,1)S(1)}, u32[]{:S(2)}, u32[]{:S(2)}) async-start(bf16[16,2,1024]{2,1,0:T(2,128)(2,1)} %broadcast_select_fusion), calls=%async_computation.1 | async-start | bytes 131072 | tf_op jit(solution)/shard_map/all_to_all | solution.py:75
  372.5 187.0 %reduce-scatter.7.cloned.1.call-start = ((), (), s32[]{:S(2)}) async-start(), calls=%async_computation.6 | async-start | bytes 8912896
  378.5 2.5 copy-start.1
Sparse Core Ops, SparseCore 0:
  348.0 102.2 reduce-scatter.4
  454.9 104.5 reduce-scatter.6
where the time goes:
time: 570 us; the launch traced here: 568 us
  waiting for transfers between devices  256 us (45%)
  local copies, waits for them, and re-layouts  223 us (39%)
  starting transfers between devices  36.9 us (6%)
  other arithmetic  25.6 us (4%)
  between operations  14.3 us (3%)
  matrix products  13.3 us (2%)
    gather x2, local copies, waits for them, and re-layouts, shards(): picked = jnp.take(node_features, wanted.reshape(devices, -1), axis=1)  192 us
    unnamed x3, waiting for transfers between devices  107 us
    all_to_all x1, waiting for transfers between devices, shards(): lax.all_to_all(picked, 'feat', split_axis=1, concat_axis=0, tiled=True)  92.8 us
    reduce_scatter x1, waiting for transfers between devices, shards(): lax.psum_scatter(jnp.concatenate([jnp.dot(own_part, grad_pre, preferred_e...  52.2 us
    all_to_all x1, starting transfers between devices, shards(): lax.all_to_all(outgoing, 'feat', split_axis=0, concat_axis=0, tiled=True)  23 us
    unnamed x20, local copies, waits for them, and re-layouts  13.7 us
  transfers between devices with their start and end apart: 5, of which 4 were waited for; matrix products, arithmetic and copies ran while one was open for 40% of the time, Pallas kernels for 0%

commit v1 on v0

--- a/solution.py
+++ b/solution.py
@@ -1,8 +1,12 @@
 import jax
 import jax.numpy as jnp
 from jax import lax
+from jax.experimental import pallas as pl
+from jax.experimental.pallas import tpu as pltpu
 from jax.sharding import PartitionSpec as P
 
+LANES = 128
+UNROLL = 4
 
 def gelu_tanh(argument):
     return jax.nn.gelu(argument, approximate=True)
@@ -28,6 +32,47 @@
         precision=lax.Precision.HIGHEST,
         preferred_element_type=jnp.float32,
     )
+
+
+def add_rows(ids_ref, table_ref, out_ref):
+    fanout = ids_ref.shape[0]
+
+    def body(group, carry):
+        for step in range(UNROLL):
+            target = group * UNROLL + step
+            terms = [table_ref[ids_ref[k, target]] for k in range(fanout)]
+            while len(terms) > 1:
+                odd = terms[-1:] if len(terms) % 2 else []
+                terms = [one + two for one, two in zip(terms[::2], terms[1::2])] + odd
+            out_ref[pl.ds(target, 1), :] = terms[0]
+        return carry
+
+    lax.fori_loop(0, out_ref.shape[0] // UNROLL, body, 0)
+
+
+def gather_sum(features, ids):
+    width, nodes = features.shape
+    fanout, targets = ids.shape
+    table = jnp.pad(features.T.astype(jnp.float32), ((0, 0), (0, LANES - width)))
+    table = table.reshape(nodes, 1, LANES)
+    step_rows = min(512, targets)
+    return pl.pallas_call(
+        add_rows,
+        grid=(targets // step_rows,),
+        out_shape=jax.ShapeDtypeStruct((targets, LANES), jnp.float32),
+        in_specs=[
+            pl.BlockSpec((fanout, step_rows), lambda b: (0, b), memory_space=pltpu.SMEM),
+            pl.BlockSpec((nodes, 1, LANES), lambda b: (0, 0, 0), pipeline_mode=pl.Buffered(1)),
+        ],
+        out_specs=pl.BlockSpec((step_rows, LANES), lambda b: (b, 0)),
+        compiler_params=pltpu.CompilerParams(vmem_limit_bytes=nodes * LANES * 4 + (8 << 20)),
+        cost_estimate=pl.CostEstimate(
+            flops=targets * fanout * LANES,
+            bytes_accessed=targets * fanout * LANES * 32,
+            transcendentals=0,
+        ),
+        name="gather_sum",
+    )(ids, table)
 
 
 def shards(
@@ -49,17 +94,42 @@
     targets = neighbors_one.shape[0]
     own_rows = targets // devices
     fanout_one = neighbors_one.shape[1]
-    block_rows = jnp.arange(targets, dtype=jnp.int32).reshape(devices, 1, own_rows)
-    fan_major = jnp.transpose(neighbors_one.reshape(devices, own_rows, fanout_one), (0, 2, 1))
-    wanted = jnp.concatenate([block_rows, fan_major], axis=1)
-    picked = jnp.take(node_features, wanted.reshape(devices, -1), axis=1)
-    arrived = lax.all_to_all(picked, "feat", split_axis=1, concat_axis=0, tiled=True)
-    full_width = arrived.shape[0]
-    arrived = arrived.reshape(full_width, fanout_one + 1, own_rows)
-    self_cols = arrived[:, 0, :]
-    mean_cols = (jnp.sum(arrived[:, 1:, :].astype(jnp.float32), axis=1) / fanout_one).astype(
-        jnp.bfloat16
-    )
+    width = node_features.shape[0]
+    pairs = devices // 2
+    half = pairs * own_rows
+    core = lax.axis_index("feat") % 2
+    swap = [(d, d ^ 1) for d in range(devices)]
+    same_core = [[2 * p + c for p in range(pairs)] for c in range(2)]
+
+    def even_odd(own, other):
+        first = jnp.where(core == 0, own, other)
+        second = jnp.where(core == 0, other, own)
+        return jnp.concatenate([first, second], axis=0)
+
+    def to_blocks(columns):
+        return lax.all_to_all(
+            columns,
+            "feat",
+            split_axis=1,
+            concat_axis=0,
+            axis_index_groups=same_core,
+            tiled=True,
+        )
+
+    def my_targets(columns):
+        cut = columns.reshape(columns.shape[0], pairs, 2, own_rows)
+        return lax.dynamic_index_in_dim(cut, core, 2, keepdims=False).reshape(-1, half)
+
+    all_out_grad = lax.all_gather(out_grad, "feat", axis=0, tiled=True)
+    partner = lax.ppermute(node_features, "feat", swap)
+    self_own = my_targets(node_features[:, :targets])
+    self_other = my_targets(partner[:, :targets])
+    self_cols = to_blocks(even_odd(self_own, self_other))
+    both = jnp.concatenate([node_features, partner], axis=0)
+    summed_one = gather_sum(both, my_targets(neighbors_one.T))
+    mean_pair = (summed_one[:, : 2 * width] / fanout_one).astype(jnp.bfloat16).T
+    mean_own, mean_other = mean_pair[:width], mean_pair[width:]
+    mean_cols = to_blocks(even_odd(mean_own, mean_other))
     pre_one = (
         contract_lead(self_cols, weight_self_one)
         + contract_lead(mean_cols, weight_neigh_one)
@@ -107,38 +177,34 @@
     grad_hidden = grad_hidden + jnp.pad(back_self, ((0, own_rows - own_seeds), (0, 0)))
     _, pull_back = jax.vjp(gelu_tanh, pre_one)
     grad_pre = pull_back(grad_hidden)[0].astype(jnp.bfloat16)
-    own_part = self_cols
-    mean_part = mean_cols
-    both_one = lax.psum_scatter(
-        jnp.concatenate(
-            [
-                jnp.dot(own_part, grad_pre, preferred_element_type=jnp.float32),
-                jnp.dot(mean_part, grad_pre, preferred_element_type=jnp.float32),
-            ],
-            axis=1,
-        ),
-        "feat",
-        scatter_dimension=0,
-        tiled=True,
-    )
-    grad_self_one = both_one[:, :hidden_width]
-    grad_neigh_one = both_one[:, hidden_width:]
-    own_part = seed_hidden
-    mean_part = mean_two
-    both_two = lax.psum_scatter(
-        jnp.concatenate(
-            [contract_lead(own_part, out_grad), contract_lead(mean_part, out_grad)], axis=1
-        ),
-        "feat",
-        scatter_dimension=0,
-        tiled=True,
-    )
+    same_grad_pre = lax.all_gather(
+        grad_pre, "feat", axis=0, axis_index_groups=same_core, tiled=True
+    )
+    for_other = jnp.dot(
+        jnp.concatenate([self_other, mean_other], axis=0),
+        same_grad_pre,
+        preferred_element_type=jnp.float32,
+    )
+    from_other = lax.ppermute(for_other, "feat", swap)
+    kept = jnp.dot(
+        jnp.concatenate([self_own, mean_own], axis=0),
+        same_grad_pre,
+        preferred_element_type=jnp.float32,
+    )
+    both_one = kept + from_other
+    seed_sides = jnp.stack([seed_hidden, mean_two]).reshape(2, own_seeds, devices, -1)
+    seed_sides = lax.all_to_all(
+        jnp.transpose(seed_sides, (2, 0, 3, 1)), "feat", split_axis=0, concat_axis=0, tiled=True
+    )
+    slice_two = seed_sides.shape[2]
+    seed_sides = jnp.transpose(seed_sides, (1, 2, 0, 3)).reshape(2 * slice_two, -1)
+    both_two = jnp.dot(seed_sides, all_out_grad, preferred_element_type=jnp.float32)
     return (
         layer_out,
-        grad_self_one,
-        grad_neigh_one,
-        both_two[:, :hidden_width],
-        both_two[:, hidden_width:],
+        both_one[:width],
+        both_one[width:],
+        both_two[:slice_two],
+        both_two[slice_two:],
     )
 
 

time: 570 us -> 208 us (0.36)
  local copies, waits for them, and re-layouts: 223 us -> 21.4 us
  waiting for transfers between devices: 256 us -> 75.6 us
  Pallas kernels: 0 us -> 37.2 us
  other arithmetic: 25.6 us -> 11.7 us
  starting transfers between devices: 36.9 us -> 29.2 us
    gather x2 -> x0, local copies, waits for them, and re-layouts: 192 us -> none  [shards(): picked = jnp.take(node_features, wanted.reshape(devices, -1), axis=1)]
    unnamed x3 -> x2, waiting for transfers between devices: 107 us -> 0.71 us
    all_to_all x1 -> x3, waiting for transfers between devices: 92.8 us -> 13.7 us  [the longest x2 6.92 us: to_blocks(): lax.all_to_all(columns, 'feat', split_axis=1, concat_axis=0, axis_index_g...]
    all_gather x0 -> x2, waiting for transfers between devices: none -> 55.8 us  [the longest x1 39.1 us: shards(): all_out_grad = lax.all_gather(out_grad, 'feat', axis=0, tiled=True)]
    reduce_scatter x1 -> x0, waiting for transfers between devices: 52.2 us -> none  [shards(): lax.psum_scatter(jnp.concatenate([jnp.dot(own_part, grad_pre, preferred_e...]
    pallas_call x0 -> x1, Pallas kernels: none -> 37.2 us  [gather_sum(): pl.pallas_call(add_rows, grid=(targets // step_rows,), out_shape=jax.Shap...]
    all_to_all x1, starting transfers between devices: 23 us -> 5.82 us  [shards(): lax.all_to_all(outgoing, 'feat', split_axis=0, concat_axis=0, tiled=True)]
    reduce_sum x1 -> x0, other arithmetic: 9.64 us -> none  [shards(): jnp.sum(arrived[:, 1:, :].astype(jnp.float32), axis=1) / fanout_one]
  transfers between devices with their start and end apart: 5 -> 9, of which waited for: 4 -> 6; matrix products, arithmetic and copies ran while one was open for 40% -> 20% of each run, Pallas kernels for 0% -> 18%
where the time goes in v1:
time: 208 us; the launch traced here: 207 us
  waiting for transfers between devices  75.6 us (36%)
  Pallas kernels  37.2 us (18%)
  starting transfers between devices  29.2 us (14%)
  local copies, waits for them, and re-layouts  21.4 us (10%)
  matrix products  17.4 us (8%)
  between operations  14.4 us (7%)
  other arithmetic  11.7 us (6%)
    all_gather x1, waiting for transfers between devices, shards(): all_out_grad = lax.all_gather(out_grad, 'feat', axis=0, tiled=True)  39.1 us
    pallas_call x1, Pallas kernels, gather_sum(): pl.pallas_call(add_rows, grid=(targets // step_rows,), out_shape=jax.Shap...  37.2 us
    all_gather x1, waiting for transfers between devices, shards(): lax.all_gather(grad_pre, 'feat', axis=0, axis_index_groups=same_core, til...  16.7 us
    all_to_all x2, starting transfers between devices, to_blocks(): lax.all_to_all(columns, 'feat', split_axis=1, concat_axis=0, axis_index_g...  9.34 us
    unnamed x43, local copies, waits for them, and re-layouts  7.43 us
    all_to_all x1, starting transfers between devices, shards(): lax.all_to_all(slot_grads.reshape(devices, slots_peer, hidden_width), 'fe...  7.26 us
    all_to_all x2, waiting for transfers between devices, to_blocks(): lax.all_to_all(columns, 'feat', split_axis=1, concat_axis=0, axis_index_g...  6.92 us
    all_to_all x1, waiting for transfers between devices, shards(): lax.all_to_all(jnp.transpose(seed_sides, (2, 0, 3, 1)), 'feat', split_axi...  6.82 us
  transfers between devices with their start and end apart: 9, of which 6 were waited for; matrix products, arithmetic and copies ran while one was open for 20% of the time, Pallas kernels for 18%

profile of v1, /device:TPU:1, one launch (start us, length us, event | category | flops | bytes accessed | tf_op | source)
XLA Modules:
  0.0 207.0 jit_solution(16398714168053080921)
XLA Ops:
  9.6 2.4 %fusion.1 = f32[64,1024,1]{1,0,2:T(8,128)S(1)} fusion(bf16[64,1024]{1,0:T(8,128)(2,1)} %param.21, bf16[1024,1024]{1,0:T(8,128)(2,1)} %param.17, f32[64]{0:T(128)S(1)} %convert_element_type.42), kind=kOutput, calls=%fused_computation.8 | convolution fusion | flops 134283264 | bytes 2490624 | tf_op jit(solution)/shard_map/dot_general | solution.py:22
  13.1 7.3 %all-to-all-start.3 = ((f32[16,2,1024]{2,1,0:T(2,128)}), f32[16,2,1024]{2,1,0:T(2,128)S(1)}, u32[]{:S(2)}, u32[]{:S(2)}) async-start(f32[16,2,1024]{2,1,0:T(2,128)} %copy.119), calls=%async_computation.3 | async-start | bytes 262144 | tf_op jit(solution)/shard_map/all_to_all | solution.py:166
  20.4 1.8 copy.111
  22.2 1.1 reshape.136
  23.6 2.7 %copy.112 = bf16[48,8192]{0,1:T(8,128)(2,1)} copy(bf16[48,8192]{1,0:T(8,128)(2,1)} %collective-permute-done) | data formatting | bytes 1572864 | tf_op jit(solution)/shard_map/ppermute | solution.py:124
  26.3 3.4 %maximum_bitcast_fusion = bf16[8192,96]{1,0:T(8,128)(2,1)S(1)} fusion(bf16[48,8192]{0,1:T(8,128)(2,1)} %copy.112, bf16[48,8192]{0,1:T(8,128)(2,1)} %copy.111), kind=kLoop, calls=%fused_computation.1 | loop fusion | flops 3145728 | bytes 3145728 | tf_op jit(solution)/shard_map/convert_element_type | solution.py:56
  29.7 2.3 %pad_convert_fusion = f32[8192,128]{1,0:T(8,128)} fusion(bf16[8192,96]{1,0:T(8,128)(2,1)S(1)} %maximum_bitcast_fusion), kind=kLoop, calls=%fused_computation.2 | loop fusion | flops 1048576 | bytes 5767168 | tf_op jit(solution)/shard_map/reshape | solution.py:57
  31.9 0.9 slice.42
  34.6 2.2 %copy-done.1 = f32[8192,128]{1,0:T(8,128)S(1)} copy-done((f32[8192,128]{1,0:T(8,128)S(1)}, f32[8192,128]{1,0:T(8,128)}, u32[]{:S(2)}) %copy-start.1) | copy-done | bytes 4194328
  36.8 37.2 %gather_sum.1 = f32[1024,128]{1,0:T(8,128)S(1)} custom-call(s32[25,1024]{1,0:T(8,128)S(1)} %bitcast.60, f32[8192,1,128]{2,1,0:T(1,128)S(1)} %bitcast.59), custom_call_target="tpu_custom_call" | custom-call | flops 3276800 | bytes 104857600 | tf_op jit(solution)/shard_map/gather_sum/pallas_call | solution.py:59
  74.1 5.4 %all-to-all-start = ((bf16[96,8,128]{2,0,1:T(8,128)(2,1)}), bf16[96,8,128]{2,0,1:T(8,128)(2,1)}, u32[]{:S(2)}, u32[]{:S(2)}) async-start(bf16[96,8,128]{2,0,1:T(8,128)(2,1)} %copy.109), calls=%async_computation | async-start | bytes 393216 | tf_op jit(solution)/shard_map/all_to_all | solution.py:110
  81.3 5.2 %all-to-all-done = bf16[96,8,128]{2,0,1:T(8,128)(2,1)} async-done(((bf16[96,8,128]{2,0,1:T(8,128)(2,1)}), bf16[96,8,128]{2,0,1:T(8,128)(2,1)}, u32[]{:S(2)}, u32[]{:S(2)}) %all-to-all-start) | async-done | bytes 196640 | tf_op jit(solution)/shard_map/all_to_all | solution.py:110
  86.5 4.0 %all-to-all-start.1 = ((bf16[96,8,128]{2,0,1:T(8,128)(2,1)}), bf16[96,8,128]{2,0,1:T(8,128)(2,1)S(1)}, u32[]{:S(2)}, u32[]{:S(2)}) async-start(bf16[96,8,128]{2,0,1:T(8,128)(2,1)} %copy.113), calls=%async_computation.1 | async-start | bytes 393216 | tf_op jit(solution)/shard_map/all_to_all | solution.py:110
  90.5 1.5 fusion.34
  93.4 1.9 fusion.33
  95.3 1.8 all-to-all-done.1
  97.8 2.1 %multiply_convert_fusion = (bf16[128,1024]{1,0:T(8,128)(2,1)S(1)}, f32[128,1024]{1,0:T(8,128)S(1)}) fusion(f32[1024]{0:T(1024)S(1)} %convert_element_type.38, f32[128,1024]{1,0:T(8,128)S(1)} %fusion.33, bf16[768,128]{1,0:T(8,128)(2,1)} %bitcast.67, bf16[768,1024]{1,0:T(8,128)(2,1)} %param.14), kind=kOutput, calls=%fused_computation.25 | convolution fusion | flops 202768384 | bytes 3084288 | tf_op jit(solution)/shard_map/dot_general | solution.py:16
  99.9 1.5 fusion.10
  103.8 5.8 %all-to-all-start.2 = ((bf16[16,2,1024]{2,1,0:T(2,128)(2,1)}), bf16[16,2,1024]{2,1,0:T(2,128)(2,1)S(1)}, u32[]{:S(2)}, u32[]{:S(2)}) async-start(bf16[16,2,1024]{2,1,0:T(2,128)(2,1)} %broadcast_select_fusion.4), calls=%async_computation.2 | async-start | bytes 131072 | tf_op jit(solution)/shard_map/all_to_all | solution.py:145
  109.8 0.9 copy.116
  110.9 5.3 %all-to-all-done.2 = bf16[16,2,1024]{2,1,0:T(2,128)(2,1)S(1)} async-done(((bf16[16,2,1024]{2,1,0:T(2,128)(2,1)}), bf16[16,2,1024]{2,1,0:T(2,128)(2,1)S(1)}, u32[]{:S(2)}, u32[]{:S(2)}) %all-to-all-start.2) | async-done | bytes 65568 | tf_op jit(solution)/shard_map/all_to_all | solution.py:145
  117.4 1.1 maximum_bitcast_fusion.1
  118.4 1.1 reshape.157
  119.6 4.8 %all-to-all-start.4 = ((bf16[16,2,4096]{2,1,0:T(2,128)(2,1)}), bf16[16,2,4096]{2,1,0:T(2,128)(2,1)S(1)}, u32[]{:S(2)}, u32[]{:S(2)}) async-start(bf16[16,2,4096]{2,1,0:T(2,128)(2,1)} %reshape.157), calls=%async_computation.4 | async-start | bytes 524288 | tf_op jit(solution)/shard_map/all_to_all | solution.py:196
  124.9 1.1 copy-done.2
  126.0 1.1 fusion.2
  127.1 6.8 %all-to-all-done.4 = bf16[16,2,4096]{2,1,0:T(2,128)(2,1)S(1)} async-done(((bf16[16,2,4096]{2,1,0:T(2,128)(2,1)}), bf16[16,2,4096]{2,1,0:T(2,128)(2,1)S(1)}, u32[]{:S(2)}, u32[]{:S(2)}) %all-to-all-start.4) | async-done | bytes 262176 | tf_op jit(solution)/shard_map/all_to_all | solution.py:196
  135.0 16.7 %all-gather.3.cloned.1.call-done = bf16[1024,1024]{1,0:T(8,128)(2,1)} async-done(((bf16[128,1024]{1,0:T(8,128)(2,1)}), bf16[1024,1024]{1,0:T(8,128)(2,1)}) %all-gather.3.cloned.1.call-update) | async-done | bytes 2097168 | tf_op jit(solution)/shard_map/all_gather | solution.py:180
  151.7 3.1 %fusion.16 = f32[96,1024]{1,0:T(8,128)} fusion(bf16[1024,1024]{1,0:T(8,128)(2,1)} %all-gather.3.cloned.1.call-done, bf16[48,1024]{0,1:T(8,128)(2,1)} %get-tuple-element.15, bf16[48,1024]{0,1:T(8,128)(2,1)S(1)} %bitcast.62), kind=kOutput, calls=%fused_computation.33 | convolution fusion | flops 201719808 | bytes 2686976 | tf_op jit(solution)/shard_map/dot_general | solution.py:183
  154.8 1.8 collective-permute-start.1
  156.5 39.1 %all-gather.5.cloned.1.call-done = bf16[1024,1024]{1,0:T(8,128)(2,1)} async-done(((bf16[64,1024]{1,0:T(8,128)(2,1)}), bf16[1024,1024]{1,0:T(8,128)(2,1)}) %all-gather.5.cloned.1.call-update) | async-done | bytes 2097168 | tf_op jit(solution)/shard_map/all_gather | solution.py:123
  195.7 2.2 %fusion.35 = f32[128,1024]{1,0:T(8,128)S(1)} fusion(bf16[128,1024]{1,0:T(8,128)(2,1)S(1)} %reshape.144, bf16[1024,1024]{1,0:T(8,128)(2,1)} %all-gather.5.cloned.1.call-done), kind=kOutput, calls=%fused_computation.69 | convolution fusion | flops 268435456 | bytes 2883584 | tf_op jit(solution)/shard_map/dot_general | solution.py:201
  (87 shorter events, 17.1 us)
Async XLA Ops:
  7.2 83.3 %copy-start = (bf16[1024,1024]{1,0:T(8,128)(2,1)S(1)}, bf16[1024,1024]{1,0:T(8,128)(2,1)}, u32[]{:S(2)}) copy-start(bf16[1024,1024]{1,0:T(8,128)(2,1)} %param.16) | copy-start | bytes 6291460
  7.2 13.2 %copy-start.4 = (bf16[48,8192]{1,0:T(8,128)(2,1)S(1)}, bf16[48,8192]{1,0:T(8,128)(2,1)}, u32[]{:S(2)}) copy-start(bf16[48,8192]{1,0:T(8,128)(2,1)} %param.11) | copy-start | bytes 2359300
  7.2 16.4 %collective-permute-start = (bf16[48,8192]{1,0:T(8,128)(2,1)}, bf16[48,8192]{1,0:T(8,128)(2,1)}, u32[]{:S(2)}, u32[]{:S(2)}) collective-permute-start(bf16[48,8192]{1,0:T(8,128)(2,1)} %param.11), channel_id=1, source_target_pairs={{0,1},{1,0},{2,3},{3,2},{4,5},{5,4},{6,7},{7,6},{8,9},{9,8},{10,11... | collective-permute-start | bytes 2359304 | tf_op jit(solution)/shard_map/ppermute | solution.py:124
  8.9 3.5 %copy-start.16 = (f32[64]{0:T(128)}, f32[64]{0:T(128)S(1)}, u32[]{:S(2)}) copy-start(f32[64]{0:T(128)S(1)} %convert_element_type.42) | copy-start | bytes 772
  9.6 2.7 %copy-start.11 = (f32[64,32]{0,1:T(8,128)}, f32[64,32]{0,1:T(8,128)S(1)}, u32[]{:S(2)}) copy-start(f32[64,32]{0,1:T(8,128)S(1)} %convert_reduce_fusion) | copy-start | bytes 24580
  13.1 61.0 %all-to-all-start.3 = ((f32[16,2,1024]{2,1,0:T(2,128)}), f32[16,2,1024]{2,1,0:T(2,128)S(1)}, u32[]{:S(2)}, u32[]{:S(2)}) async-start(f32[16,2,1024]{2,1,0:T(2,128)} %copy.119), calls=%async_computation.3 | async-start | bytes 262144 | tf_op jit(solution)/shard_map/all_to_all | solution.py:166
  34.6 2.2 %copy-start.1 = (f32[8192,128]{1,0:T(8,128)S(1)}, f32[8192,128]{1,0:T(8,128)}, u32[]{:S(2)}) copy-start(f32[8192,128]{1,0:T(8,128)} %pad_convert_fusion) | copy-start | bytes 12582916
  74.0 16.5 %copy-start.5 = (bf16[64,1024]{1,0:T(8,128)(2,1)S(1)}, bf16[64,1024]{1,0:T(8,128)(2,1)}, u32[]{:S(2)}) copy-start(bf16[64,1024]{1,0:T(8,128)(2,1)} %param.21) | copy-start | bytes 393220
  74.1 12.4 %all-to-all-start = ((bf16[96,8,128]{2,0,1:T(8,128)(2,1)}), bf16[96,8,128]{2,0,1:T(8,128)(2,1)}, u32[]{:S(2)}, u32[]{:S(2)}) async-start(bf16[96,8,128]{2,0,1:T(8,128)(2,1)} %copy.109), calls=%async_computation | async-start | bytes 393216 | tf_op jit(solution)/shard_map/all_to_all | solution.py:110
  80.4 11.6 %copy-start.13 = (bf16[1024]{0:T(1024)(128)(2,1)S(1)}, bf16[1024]{0:T(1024)(128)(2,1)}, u32[]{:S(2)}) copy-start(bf16[1024]{0:T(1024)(128)(2,1)} %param.15) | copy-start | bytes 6148
  80.4 11.6 %copy-start.14 = (s32[1,16,2]{1,2,0:T(2,128)S(1)}, s32[1,16,2]{1,2,0:T(2,128)}, u32[]{:S(2)}) copy-start(s32[1,16,2]{1,2,0:T(2,128)} %param.18) | copy-start | bytes 388
  86.5 10.6 %all-to-all-start.1 = ((bf16[96,8,128]{2,0,1:T(8,128)(2,1)}), bf16[96,8,128]{2,0,1:T(8,128)(2,1)S(1)}, u32[]{:S(2)}, u32[]{:S(2)}) async-start(bf16[96,8,128]{2,0,1:T(8,128)(2,1)} %copy.113), calls=%async_computation.1 | async-start | bytes 393216 | tf_op jit(solution)/shard_map/all_to_all | solution.py:110
  90.5 61.2 %all-gather.3.cloned.1.call-start = ((), (), s32[]{:S(2)}) async-start(), calls=%async_computation.5 | async-start | bytes 2359296 | tf_op jit(solution)/shard_map/all_gather | solution.py:180
  95.3 4.6 %copy-start.9 = (f32[64,1024]{1,0:T(8,128)S(1)}, f32[64,1024]{1,0:T(8,128)}, u32[]{:S(2)}) copy-start(f32[64,1024]{1,0:T(8,128)} %fusion.34) | copy-start | bytes 786436
  97.1 0.7 copy-start.8
  97.8 2.1 %copy-start.10 = (f32[32,1024]{1,0:T(8,128)S(1)}, f32[32,1024]{1,0:T(8,128)}, u32[]{:S(2)}) copy-start(f32[32,1024]{1,0:T(8,128)} %reshape.142) | copy-start | bytes 393220
  97.8 2.1 %copy-start.15 = (s32[32]{0:T(128)S(1)}, s32[32]{0:T(128)}, u32[]{:S(2)}) copy-start(s32[32]{0:T(128)} %reshape_squeeze.9) | copy-start | bytes 388
  101.4 14.9 %copy-start.12 = (f32[64,32]{0,1:T(8,128)S(1)}, f32[64,32]{0,1:T(8,128)}, u32[]{:S(2)}) copy-start(f32[64,32]{0,1:T(8,128)} %copy-done.11) | copy-start | bytes 24580
  101.4 14.9 %copy-start.17 = (f32[64]{0:T(128)S(1)}, f32[64]{0:T(128)}, u32[]{:S(2)}) copy-start(f32[64]{0:T(128)} %copy-done.16) | copy-start | bytes 772
  101.4 94.2 %all-gather.5.cloned.1.call-start = ((), (), s32[]{:S(2)}) async-start(), calls=%async_computation.6 | async-start | bytes 2228224 | tf_op jit(solution)/shard_map/all_gather | solution.py:123
  103.8 12.4 %all-to-all-start.2 = ((bf16[16,2,1024]{2,1,0:T(2,128)(2,1)}), bf16[16,2,1024]{2,1,0:T(2,128)(2,1)S(1)}, u32[]{:S(2)}, u32[]{:S(2)}) async-start(bf16[16,2,1024]{2,1,0:T(2,128)(2,1)} %broadcast_select_fusion.4), calls=%async_computation.2 | async-start | bytes 131072 | tf_op jit(solution)/shard_map/all_to_all | solution.py:145
  119.6 14.3 %all-to-all-start.4 = ((bf16[16,2,4096]{2,1,0:T(2,128)(2,1)}), bf16[16,2,4096]{2,1,0:T(2,128)(2,1)S(1)}, u32[]{:S(2)}, u32[]{:S(2)}) async-start(bf16[16,2,4096]{2,1,0:T(2,128)(2,1)} %reshape.157), calls=%async_computation.4 | async-start | bytes 524288 | tf_op jit(solution)/shard_map/all_to_all | solution.py:196
  124.4 1.6 copy-start.2
  154.8 43.9 %copy-start.6 = (bf16[48,8,1,128]{0,3,1,2:T(8,128)(2,1)S(1)}, bf16[48,8,1,128]{0,3,1,2:T(8,128)(2,1)}, u32[]{:S(2)}) copy-start(bf16[48,8,1,128]{0,3,1,2:T(8,128)(2,1)} %copy.116) | copy-start | bytes 294916
  154.8 44.0 %copy-start.7 = (bf16[48,1024]{0,1:T(8,128)(2,1)S(1)}, bf16[48,1024]{0,1:T(8,128)(2,1)}, u32[]{:S(2)}) copy-start(bf16[48,1024]{0,1:T(8,128)(2,1)} %get-tuple-element.12) | copy-start | bytes 294916
  154.8 43.9 %collective-permute-start.1 = (f32[96,1024]{1,0:T(8,128)}, f32[96,1024]{1,0:T(8,128)S(1)}, u32[]{:S(2)}, u32[]{:S(2)}) collective-permute-start(f32[96,1024]{1,0:T(8,128)} %fusion.16), channel_id=1, source_target_pairs={{0,1},{1,0},{2,3},{3,2},{4,5},{5,4},{6,7},{7,6},{8,9},{9,8},{10,11... | collective-permute-start | bytes 1179656 | tf_op jit(solution)/shard_map/ppermute | solution.py:188
  195.7 3.0 %copy-start.3 = (bf16[1024,1024]{1,0:T(8,128)(2,1)S(1)}, bf16[1024,1024]{1,0:T(8,128)(2,1)}, u32[]{:S(2)}) copy-start(bf16[1024,1024]{1,0:T(8,128)(2,1)} %all-gather.3.cloned.1.call-done) | copy-start | bytes 6291460
Sparse Core Ops, SparseCore 0:
  101.5 50.0 all-gather.2
  153.8 41.8 all-gather.4

commit v2 on v1

--- a/solution.py
+++ b/solution.py
@@ -34,13 +34,27 @@
     )
 
 
-def add_rows(ids_ref, table_ref, out_ref):
+def add_rows(ids_ref, own_ref, partner_ref, out_ref, table_ref):
     fanout = ids_ref.shape[0]
+    width, nodes = own_ref.shape
+
+    @pl.when(pl.program_id(0) == 0)
+    def fill_table():
+        blank = jnp.zeros((LANES - 2 * width, LANES), jnp.float32)
+
+        def turn(block, carry):
+            spot = pl.ds(pl.multiple_of(block * LANES, LANES), LANES)
+            own = own_ref[:, spot].astype(jnp.float32)
+            partner = partner_ref[:, spot].astype(jnp.float32)
+            table_ref[spot, :] = jnp.concatenate([own, partner, blank], axis=0).T
+            return carry
+
+        lax.fori_loop(0, nodes // LANES, turn, 0, unroll=4)
 
     def body(group, carry):
         for step in range(UNROLL):
             target = group * UNROLL + step
-            terms = [table_ref[ids_ref[k, target]] for k in range(fanout)]
+            terms = [table_ref[pl.ds(ids_ref[k, target], 1), :] for k in range(fanout)]
             while len(terms) > 1:
                 odd = terms[-1:] if len(terms) % 2 else []
                 terms = [one + two for one, two in zip(terms[::2], terms[1::2])] + odd
@@ -50,29 +64,32 @@
     lax.fori_loop(0, out_ref.shape[0] // UNROLL, body, 0)
 
 
-def gather_sum(features, ids):
-    width, nodes = features.shape
+def gather_sum(own, partner, ids):
+    width, nodes = own.shape
     fanout, targets = ids.shape
-    table = jnp.pad(features.T.astype(jnp.float32), ((0, 0), (0, LANES - width)))
-    table = table.reshape(nodes, 1, LANES)
     step_rows = min(512, targets)
+    whole = pl.BlockSpec((width, nodes), lambda b: (0, 0), pipeline_mode=pl.Buffered(1))
     return pl.pallas_call(
         add_rows,
         grid=(targets // step_rows,),
         out_shape=jax.ShapeDtypeStruct((targets, LANES), jnp.float32),
         in_specs=[
             pl.BlockSpec((fanout, step_rows), lambda b: (0, b), memory_space=pltpu.SMEM),
-            pl.BlockSpec((nodes, 1, LANES), lambda b: (0, 0, 0), pipeline_mode=pl.Buffered(1)),
+            whole,
+            whole,
         ],
         out_specs=pl.BlockSpec((step_rows, LANES), lambda b: (b, 0)),
-        compiler_params=pltpu.CompilerParams(vmem_limit_bytes=nodes * LANES * 4 + (8 << 20)),
+        scratch_shapes=[pltpu.VMEM((nodes, LANES), jnp.float32)],
+        compiler_params=pltpu.CompilerParams(
+            vmem_limit_bytes=nodes * (LANES + width) * 4 + (8 << 20)
+        ),
         cost_estimate=pl.CostEstimate(
             flops=targets * fanout * LANES,
             bytes_accessed=targets * fanout * LANES * 32,
             transcendentals=0,
         ),
         name="gather_sum",
-    )(ids, table)
+    )(ids, own, partner)
 
 
 def shards(
@@ -121,14 +138,18 @@
         return lax.dynamic_index_in_dim(cut, core, 2, keepdims=False).reshape(-1, half)
 
     all_out_grad = lax.all_gather(out_grad, "feat", axis=0, tiled=True)
-    partner = lax.ppermute(node_features, "feat", swap)
-    self_own = my_targets(node_features[:, :targets])
-    self_other = my_targets(partner[:, :targets])
-    self_cols = to_blocks(even_odd(self_own, self_other))
-    both = jnp.concatenate([node_features, partner], axis=0)
-    summed_one = gather_sum(both, my_targets(neighbors_one.T))
-    mean_pair = (summed_one[:, : 2 * width] / fanout_one).astype(jnp.bfloat16).T
-    mean_own, mean_other = mean_pair[:width], mean_pair[width:]
+    spare = -width % 16
+    features = jnp.pad(node_features, ((0, spare), (0, 0)))
+    partner = lax.ppermute(features, "feat", swap)
+    self_all = node_features[:, :targets]
+    self_cols = lax.all_to_all(self_all, "feat", split_axis=1, concat_axis=0, tiled=True)
+    self_own = my_targets(self_all)
+    self_other = my_targets(partner[:width, :targets])
+    features, self_cols = lax.optimization_barrier((features, self_cols))
+    summed_one = gather_sum(features, partner, my_targets(neighbors_one.T))
+    mean_pair = (summed_one[:, : 2 * (width + spare)] / fanout_one).astype(jnp.bfloat16).T
+    mean_pair, all_out_grad = lax.optimization_barrier((mean_pair, all_out_grad))
+    mean_own, mean_other = mean_pair[:width], mean_pair[width + spare :][:width]
     mean_cols = to_blocks(even_odd(mean_own, mean_other))
     pre_one = (
         contract_lead(self_cols, weight_self_one)
@@ -139,9 +160,13 @@
     peer_rows = send_rows[0]
     slots_peer = peer_rows.shape[1]
     slot_total = devices * slots_peer
-    outgoing = jnp.take(hidden_one, peer_rows.reshape(-1), axis=0).reshape(
-        devices, slots_peer, hidden_width
-    )
+    row_hits = (
+        peer_rows.reshape(-1)[:, None] == jnp.arange(own_rows, dtype=jnp.int32)[None, :]
+    ).astype(jnp.float32)
+    sent_rows = jnp.dot(
+        row_hits.astype(jnp.bfloat16), hidden_one, preferred_element_type=jnp.float32
+    ).astype(jnp.bfloat16)
+    outgoing = sent_rows.reshape(devices, slots_peer, hidden_width)
     incoming = lax.all_to_all(outgoing, "feat", split_axis=0, concat_axis=0, tiled=True)
     fanout_two = neighbors_two.shape[1]
     keep_mask = jnp.arange(fanout_two, dtype=jnp.int32)[None, :] < degree_two[:, None]
@@ -149,6 +174,8 @@
     slot_hits = (neighbors_two[:, :, None] == slot_ids[None, None, :]) & keep_mask[:, :, None]
     ref_count = jnp.sum(slot_hits.astype(jnp.float32), axis=1)
     degree_float = degree_two.astype(jnp.float32)[:, None]
+    slot_out = exact_lead(ref_count / degree_float, out_grad.astype(jnp.float32))
+    all_slot_out = lax.all_gather(slot_out.astype(jnp.bfloat16), "feat", axis=0, tiled=True)
     summed_two = jnp.dot(
         ref_count.astype(jnp.bfloat16),
         incoming.reshape(slot_total, hidden_width),
@@ -170,41 +197,57 @@
         concat_axis=0,
         tiled=True,
     )
-    row_hits = (
-        peer_rows.reshape(-1)[:, None] == jnp.arange(own_rows, dtype=jnp.int32)[None, :]
-    ).astype(jnp.float32)
     grad_hidden = exact_lead(row_hits, returned.reshape(slot_total, hidden_width))
     grad_hidden = grad_hidden + jnp.pad(back_self, ((0, own_rows - own_seeds), (0, 0)))
     _, pull_back = jax.vjp(gelu_tanh, pre_one)
     grad_pre = pull_back(grad_hidden)[0].astype(jnp.bfloat16)
-    same_grad_pre = lax.all_gather(
-        grad_pre, "feat", axis=0, axis_index_groups=same_core, tiled=True
-    )
-    for_other = jnp.dot(
-        jnp.concatenate([self_other, mean_other], axis=0),
-        same_grad_pre,
-        preferred_element_type=jnp.float32,
-    )
-    from_other = lax.ppermute(for_other, "feat", swap)
-    kept = jnp.dot(
-        jnp.concatenate([self_own, mean_own], axis=0),
-        same_grad_pre,
-        preferred_element_type=jnp.float32,
-    )
-    both_one = kept + from_other
-    seed_sides = jnp.stack([seed_hidden, mean_two]).reshape(2, own_seeds, devices, -1)
-    seed_sides = lax.all_to_all(
-        jnp.transpose(seed_sides, (2, 0, 3, 1)), "feat", split_axis=0, concat_axis=0, tiled=True
-    )
-    slice_two = seed_sides.shape[2]
-    seed_sides = jnp.transpose(seed_sides, (1, 2, 0, 3)).reshape(2 * slice_two, -1)
-    both_two = jnp.dot(seed_sides, all_out_grad, preferred_element_type=jnp.float32)
+    order = list(range(0, pairs, 2)) + list(range(1, pairs, 2))[::-1]
+    spots = jnp.asarray(order, jnp.int32)
+    mine = jnp.asarray([order.index(p) for p in range(pairs)], jnp.int32)[
+        lax.axis_index("feat") // 2
+    ]
+    onward = [
+        (2 * order[i] + c, 2 * order[(i + 1) % pairs] + c) for i in range(pairs) for c in range(2)
+    ]
+    back = [(there, here) for here, there in onward]
+    left = jnp.concatenate([self_other, mean_other, self_own, mean_own], axis=0)
+    left = jnp.transpose(left.reshape(4 * width, pairs, own_rows), (1, 0, 2))
+
+    def term(hop, block):
+        owner = spots[lax.rem(mine + hop + pairs, pairs)]
+        return jnp.dot(
+            lax.dynamic_index_in_dim(left, owner, 0, keepdims=False),
+            block,
+            preferred_element_type=jnp.float32,
+        )
+
+    total = term(0, grad_pre)
+    going, coming = grad_pre, grad_pre
+    for hop in range(1, (pairs + 1) // 2):
+        going = lax.ppermute(going, "feat", onward)
+        coming = lax.ppermute(coming, "feat", back)
+        total = total + term(-hop, going) + term(hop, coming)
+    if pairs % 2 == 0:
+        cut = own_rows // 2
+        first = lax.ppermute(going[:cut], "feat", onward)
+        second = lax.ppermute(coming[cut:], "feat", back)
+        total = total + term(pairs // 2, jnp.concatenate([first, second], axis=0))
+    from_other = lax.ppermute(total[: 2 * width], "feat", swap)
+    both_one = total[2 * width :] + from_other
+
+    side_rows = jnp.concatenate([seed_hidden, sent_rows], axis=0)
+    side_rows = jnp.transpose(side_rows.reshape(own_seeds + slot_total, devices, -1), (1, 0, 2))
+    side_rows = lax.all_to_all(side_rows, "feat", split_axis=0, concat_axis=0, tiled=True)
+    slice_two = side_rows.shape[2]
+    seed_cols = side_rows[:, :own_seeds].reshape(-1, slice_two)
+    sent_cols = side_rows[:, own_seeds:].reshape(devices, devices, slots_peer, slice_two)
+    sent_cols = jnp.transpose(sent_cols, (1, 0, 2, 3)).reshape(-1, slice_two)
     return (
         layer_out,
         both_one[:width],
         both_one[width:],
-        both_two[:slice_two],
-        both_two[slice_two:],
+        contract_lead(seed_cols, all_out_grad),
+        contract_lead(sent_cols, all_slot_out),
     )
 
 

time: 208 us -> 181 us (0.87)
  waiting for transfers between devices: 75.6 us -> 16.2 us
  between operations: 14.4 us -> 34.7 us
  matrix products: 17.4 us -> 28.2 us
  starting transfers between devices: 29.2 us -> 40 us
  other arithmetic: 11.7 us -> 5.19 us
  Pallas kernels: 37.2 us -> 34.1 us
    all_gather x1, waiting for transfers between devices: 39.1 us -> 0.01 us  [shards(): all_out_grad = lax.all_gather(out_grad, 'feat', axis=0, tiled=True)]
    all_gather x1, waiting for transfers between devices: 16.7 us -> 0.01 us  [shards(): lax.all_gather(slot_out.astype(jnp.bfloat16), 'feat', axis=0, tiled=True)]
    ppermute x2 -> x10, starting transfers between devices: 1.89 us -> 11 us  [the longest x3 3.1 us: shards(): coming = lax.ppermute(coming, 'feat', back)]
    ppermute x2 -> x10, waiting for transfers between devices: 0.01 us -> 8.5 us  [the longest x3 2.69 us: shards(): coming = lax.ppermute(coming, 'feat', back)]
    unnamed x43 -> x39, local copies, waits for them, and re-layouts: 7.43 us -> 1.53 us
    dot_general x2 -> x4, matrix products: 4.03 us -> 9.77 us  [contract_lead(): lax.dot_general(left_side, right_side, (((0,), (0,)), ((), ())), preferre...]
    all_to_all x2 -> x1, waiting for transfers between devices: 6.92 us -> 1.33 us  [to_blocks(): lax.all_to_all(columns, 'feat', split_axis=1, concat_axis=0, axis_index_g...]
    all_to_all x1 -> x2, starting transfers between devices: 4.8 us -> 10.3 us  [the longest x1 6.02 us: shards(): lax.all_to_all(self_all, 'feat', split_axis=1, concat_axis=0, tiled=True)]
  transfers between devices with their start and end apart: 9 -> 17, of which waited for: 6 -> 7; matrix products, arithmetic and copies ran while one was open for 20% -> 29% of each run, Pallas kernels for 18% -> 19%
where the time goes in v2:
time: 181 us; the launch traced here: 179 us
  starting transfers between devices  40 us (22%)
  between operations  34.7 us (19%)
  Pallas kernels  34.1 us (19%)
  matrix products  28.2 us (16%)
  local copies, waits for them, and re-layouts  20.8 us (11%)
  waiting for transfers between devices  16.2 us (9%)
  other arithmetic  5.19 us (3%)
    pallas_call x1, Pallas kernels, gather_sum(): pl.pallas_call(add_rows, grid=(targets // step_rows,), out_shape=jax.Shap...  34.1 us
    dot_general x4, matrix products, contract_lead(): lax.dot_general(left_side, right_side, (((0,), (0,)), ((), ())), preferre...  9.77 us
    dot_general x8, matrix products, term(): jnp.dot(lax.dynamic_index_in_dim(left, owner, 0, keepdims=False), block,...  8.05 us
    all_to_all x1, starting transfers between devices, shards(): lax.all_to_all(slot_grads.reshape(devices, slots_peer, hidden_width), 'fe...  7.38 us
    all_to_all x1, starting transfers between devices, shards(): lax.all_to_all(self_all, 'feat', split_axis=1, concat_axis=0, tiled=True)  6.02 us
    all_to_all x1, starting transfers between devices, shards(): lax.all_to_all(outgoing, 'feat', split_axis=0, concat_axis=0, tiled=True)  5.88 us
    all_to_all x1, starting transfers between devices, to_blocks(): lax.all_to_all(columns, 'feat', split_axis=1, concat_axis=0, axis_index_g...  5.36 us
    reshape x3, local copies, waits for them, and re-layouts, my_targets(): cut = columns.reshape(columns.shape[0], pairs, 2, own_rows)  4.35 us
  transfers between devices with their start and end apart: 17, of which 7 were waited for; matrix products, arithmetic and copies ran while one was open for 29% of the time, Pallas kernels for 19%

profile of v2, /device:TPU:1, one launch (start us, length us, event | category | flops | bytes accessed | tf_op | source)
XLA Modules:
  0.0 179.1 jit_solution(17394064727537041989)
XLA Ops:
  10.2 2.4 %fusion.4 = f32[64,1024,1]{1,0,2:T(8,128)S(1)} fusion(bf16[64,1024]{1,0:T(8,128)(2,1)} %param.23, bf16[1024,1024]{1,0:T(8,128)(2,1)} %param.19, f32[64]{0:T(128)S(1)} %convert_element_type.50), kind=kOutput, calls=%fused_computation.11 | convolution fusion | flops 134283264 | bytes 2490624 | tf_op jit(solution)/shard_map/dot_general | solution.py:22
  13.6 7.4 %all-to-all-start.3 = ((f32[16,2,1024]{2,1,0:T(2,128)}), f32[16,2,1024]{2,1,0:T(2,128)S(1)}, u32[]{:S(2)}, u32[]{:S(2)}) async-start(f32[16,2,1024]{2,1,0:T(2,128)} %copy.74), calls=%async_computation.3 | async-start | bytes 262144 | tf_op jit(solution)/shard_map/all_to_all | solution.py:193
  21.9 1.7 fusion.52
  40.1 1.8 %reshape.120 = s32[25,8,2,128]{3,2,1,0:T(2,128)} reshape(s32[25,2048]{1,0:T(8,128)} %bitcast.123) | data formatting | bytes 409600 | tf_op jit(solution)/shard_map/reshape | solution.py:137
  43.3 6.0 %all-to-all-start = ((bf16[48,16,128]{2,0,1:T(8,128)(2,1)}), bf16[48,16,128]{2,0,1:T(8,128)(2,1)S(1)}, u32[]{:S(2)}, u32[]{:S(2)}) async-start(bf16[48,16,128]{2,0,1:T(8,128)(2,1)} %bitcast.106), calls=%async_computation | async-start | bytes 393216 | tf_op jit(solution)/shard_map/all_to_all | solution.py:145
  50.4 1.7 reshape.125
  57.4 1.5 fusion.57
  59.6 2.7 %fusion.56 = f32[128,1024]{1,0:T(8,128)} fusion(bf16[768,128]{1,0:T(8,128)(2,1)S(1)} %bitcast.115, bf16[768,1024]{1,0:T(8,128)(2,1)} %param.15), kind=kOutput, calls=%fused_computation.96 | convolution fusion | flops 201326592 | bytes 2293760 | tf_op jit(solution)/shard_map/dot_general | solution.py:16
  62.3 34.1 %gather_sum.1 = f32[1024,128]{1,0:T(8,128)S(1)} custom-call(s32[25,1024]{1,0:T(8,128)S(1)} %bitcast.110, bf16[48,8192]{1,0:T(8,128)(2,1)S(1)} %copy-done.1, bf16[48,8192]{1,0:T(8,128)(2,1)S(1)} %collective-permute-done.partner_ref), custom_call_target="tpu_custom_call" | custom-call | flops 3276800 | bytes 104857600 | tf_op jit(solution)/shard_map/gather_sum/pallas_call | solution.py:72
  99.1 5.4 %all-to-all-start.1 = ((bf16[96,8,128]{2,0,1:T(8,128)(2,1)}), bf16[96,8,128]{2,0,1:T(8,128)(2,1)}, u32[]{:S(2)}, u32[]{:S(2)}) async-start(bf16[96,8,128]{2,0,1:T(8,128)(2,1)} %copy.67), calls=%async_computation.1 | async-start | bytes 393216 | tf_op jit(solution)/shard_map/all_to_all | solution.py:127
  104.5 1.5 constant_dynamic-slice_fusion.8
  108.6 1.6 constant_dynamic-slice_fusion.2
  110.2 1.3 all-to-all-done.1
  111.5 2.1 %multiply_convert_fusion = (bf16[128,1024]{1,0:T(8,128)(2,1)S(1)}, f32[128,1024]{1,0:T(8,128)S(1)}) fusion(f32[1024]{0:T(1024)S(1)} %convert_element_type.43, f32[128,1024]{1,0:T(8,128)S(1)} %copy-done.3, bf16[768,128]{1,0:T(8,128)(2,1)} %bitcast.6, bf16[768,1024]{1,0:T(8,128)(2,1)} %param.16), kind=kOutput, calls=%fused_computation.29 | convolution fusion | flops 202768384 | bytes 3084288 | tf_op jit(solution)/shard_map/dot_general | solution.py:16
  113.6 1.8 %fusion.13 = bf16[128,1024]{1,0:T(8,128)(2,1)S(1)} fusion(f32[128,1024]{1,0:T(8,128)S(1)} %get-tuple-element.38, f32[32,1024]{1,0:T(8,128)} %reshape.126, f32[64,1024]{1,0:T(8,128)} %fusion.57, s32[32]{0:T(128)S(1)} %eq.38), kind=kOutput, calls=%fused_computation.26 | convolution fusion | flops 53088256 | bytes 1179776 | tf_op jit(solution)/shard_map/dot_general | solution.py:28
  118.2 5.9 %all-to-all-start.2 = ((bf16[16,2,1024]{2,1,0:T(2,128)(2,1)}), bf16[16,2,1024]{2,1,0:T(2,128)(2,1)S(1)}, u32[]{:S(2)}, u32[]{:S(2)}) async-start(bf16[16,2,1024]{2,1,0:T(2,128)(2,1)} %reshape.122), calls=%async_computation.2 | async-start | bytes 131072 | tf_op jit(solution)/shard_map/all_to_all | solution.py:170
  126.1 4.1 %all-to-all-done.2 = bf16[16,2,1024]{2,1,0:T(2,128)(2,1)S(1)} async-done(((bf16[16,2,1024]{2,1,0:T(2,128)(2,1)}), bf16[16,2,1024]{2,1,0:T(2,128)(2,1)S(1)}, u32[]{:S(2)}, u32[]{:S(2)}) %all-to-all-start.2) | async-done | bytes 65568 | tf_op jit(solution)/shard_map/all_to_all | solution.py:170
  130.2 4.3 %all-to-all-start.4 = ((bf16[16,96,64]{1,2,0:T(8,128)(2,1)}), bf16[16,96,64]{1,2,0:T(8,128)(2,1)S(1)}, u32[]{:S(2)}, u32[]{:S(2)}) async-start(bf16[16,96,64]{1,2,0:T(8,128)(2,1)} %bitcast.31), calls=%async_computation.4 | async-start | bytes 524288 | tf_op jit(solution)/shard_map/all_to_all | solution.py:240
  134.6 2.9 %fusion.5 = bf16[64,1024]{1,0:T(8,128)(2,1)} fusion(f32[64,1024]{1,0:T(8,128)S(1)} %fusion.50, bf16[1024,1024]{1,0:T(8,128)(2,1)} %param.19, bf16[32,1024]{1,0:T(8,128)(2,1)S(1)} %reshape.123, f32[64]{0:T(128)S(1)} %convert_element_type.50, f32[64,32]{0,1:T(8,128)S(1)} %convert_reduce_fusion), kind=kOutput, calls=%fused_computation.14 | convolution fusion | flops 138676224 | bytes 2564352 | tf_op jit(solution)/shard_map/dot_general | solution.py:186
  137.5 1.4 collective-permute-start.4
  138.9 1.5 convolution_add_fusion.3
  140.5 2.1 %convolution_add_fusion.2 = f32[192,1024]{1,0:T(8,128)} fusion(f32[192,1024]{1,0:T(8,128)S(1)} %convolution_add_fusion.3, bf16[128,1024]{1,0:T(8,128)(2,1)} %collective-permute-done.2, bf16[192,1,128]{2,1,0:T(2,128)(2,1)S(1)} %copy-done.12), kind=kOutput, calls=%fused_computation.5 | convolution fusion | flops 50528256 | bytes 1884160 | tf_op jit(solution)/shard_map/dot_general | solution.py:218
  142.5 1.5 all-to-all-done.4
  144.5 2.7 %collective-permute-done.4 = bf16[128,1024]{1,0:T(8,128)(2,1)} collective-permute-done((bf16[128,1024]{1,0:T(8,128)(2,1)}, bf16[128,1024]{1,0:T(8,128)(2,1)}, u32[]{:S(2)}, u32[]{:S(2)}) %collective-permute-start.4) | collective-permute-done | bytes 262176 | tf_op jit(solution)/shard_map/ppermute | solution.py:228
  147.6 1.9 %collective-permute-start.5 = (bf16[128,1024]{1,0:T(8,128)(2,1)}, bf16[128,1024]{1,0:T(8,128)(2,1)S(1)}, u32[]{:S(2)}, u32[]{:S(2)}) collective-permute-start(bf16[128,1024]{1,0:T(8,128)(2,1)} %collective-permute-done.3), channel_id=1, source_target_pairs={{0,4},{1,5},{4,8},{5,9},{8,12},{9,13},{12,14},{13,15},{14,10},{15,... | collective-permute-start | bytes 786440 | tf_op jit(solution)/shard_map/ppermute | solution.py:227
  152.1 2.4 %collective-permute-done.5 = bf16[128,1024]{1,0:T(8,128)(2,1)S(1)} collective-permute-done((bf16[128,1024]{1,0:T(8,128)(2,1)}, bf16[128,1024]{1,0:T(8,128)(2,1)S(1)}, u32[]{:S(2)}, u32[]{:S(2)}) %collective-permute-start.5) | collective-permute-done | bytes 262176 | tf_op jit(solution)/shard_map/ppermute | solution.py:227
  154.5 2.1 %collective-permute-start.7 = (bf16[64,1024]{1,0:T(8,128)(2,1)S(1)}, bf16[64,1024]{1,0:T(8,128)(2,1)S(1)}, u32[]{:S(2)}, u32[]{:S(2)}) collective-permute-start(bf16[64,1024]{1,0:T(8,128)(2,1)S(1)} %slice.59), channel_id=1, source_target_pairs={{0,4},{1,5},{4,8},{5,9},{8,12},{9,13},{12,14},{13,15},{14,10},{15,... | collective-permute-start | bytes 393224 | tf_op jit(solution)/shard_map/ppermute | solution.py:232
  157.5 2.0 %collective-permute-done.7 = bf16[64,1024]{1,0:T(8,128)(2,1)S(1)} collective-permute-done((bf16[64,1024]{1,0:T(8,128)(2,1)S(1)}, bf16[64,1024]{1,0:T(8,128)(2,1)S(1)}, u32[]{:S(2)}, u32[]{:S(2)}) %collective-permute-start.7) | collective-permute-done | bytes 131104 | tf_op jit(solution)/shard_map/ppermute | solution.py:232
  159.5 1.4 collective-permute-done.8
  162.2 2.9 %collective-permute-start.9 = (f32[96,1024]{1,0:T(8,128)}, f32[96,1024]{1,0:T(8,128)}, u32[]{:S(2)}, u32[]{:S(2)}) collective-permute-start(f32[96,1024]{1,0:T(8,128)} %slice.62), channel_id=1, source_target_pairs={{0,1},{1,0},{2,3},{3,2},{4,5},{5,4},{6,7},{7,6},{8,9},{9,8},{10,11... | collective-permute-start | bytes 1179656 | tf_op jit(solution)/shard_map/ppermute | solution.py:235
  165.1 2.2 %fusion.59 = f32[64,1024]{1,0:T(8,128)} fusion(bf16[512,64]{1,0:T(8,128)(2,1)S(1)} %bitcast.118, bf16[512,1024]{1,0:T(8,128)(2,1)} %all-gather.5.cloned.1.call-done), kind=kOutput, calls=%fused_computation.99 | convolution fusion | flops 67108864 | bytes 1376256 | tf_op jit(solution)/shard_map/dot_general | solution.py:16
  167.7 2.8 %fusion.58 = f32[64,1024]{1,0:T(8,128)} fusion(bf16[1024,64]{0,1:T(8,128)(2,1)S(1)} %reshape.128, bf16[1024,1024]{1,0:T(8,128)(2,1)} %all-gather.3.cloned.1.call-done), kind=kOutput, calls=%fused_computation.98 | convolution fusion | flops 134217728 | bytes 2490368 | tf_op jit(solution)/shard_map/dot_general | solution.py:16
  (104 shorter events, 27.4 us)
Async XLA Ops:
  7.2 50.2 %copy-start = (bf16[1024,1024]{1,0:T(8,128)(2,1)S(1)}, bf16[1024,1024]{1,0:T(8,128)(2,1)}, u32[]{:S(2)}) copy-start(bf16[1024,1024]{1,0:T(8,128)(2,1)} %param.18) | copy-start | bytes 6291460
  7.2 13.9 %copy-start.4 = (bf16[64,1024]{1,0:T(8,128)(2,1)S(1)}, bf16[64,1024]{1,0:T(8,128)(2,1)}, u32[]{:S(2)}) copy-start(bf16[64,1024]{1,0:T(8,128)(2,1)} %param.23) | copy-start | bytes 393220
  7.2 90.1 %all-gather.3.cloned.1.call-start = ((), (), s32[]{:S(2)}) async-start(), calls=%async_computation.5 | async-start | bytes 2228224 | tf_op jit(solution)/shard_map/all_gather | solution.py:140
  7.9 54.3 %collective-permute-start = (bf16[48,8192]{1,0:T(8,128)(2,1)}, bf16[48,8192]{1,0:T(8,128)(2,1)S(1)}, u32[]{:S(2)}, u32[]{:S(2)}) collective-permute-start(bf16[48,8192]{1,0:T(8,128)(2,1)} %own_ref), channel_id=1, source_target_pairs={{0,1},{1,0},{2,3},{3,2},{4,5},{5,4},{6,7},{7,6},{8,9},{9,8},{10,11... | collective-permute-start | bytes 2359304 | tf_op jit(solution)/shard_map/ppermute | solution.py:143
  10.1 13.5 %copy-start.16 = (s32[8]{0:T(128)S(1)}, s32[8]{0:T(128)}, u32[]{:S(2)}) copy-start(s32[8]{0:T(128)} %constant.128.clone) | copy-start | bytes 100
  10.1 19.3 %copy-start.13 = (s32[8]{0:T(128)S(1)}, s32[8]{0:T(128)}, u32[]{:S(2)}) copy-start(s32[8]{0:T(128)} %constant.127.clone) | copy-start | bytes 100
  12.9 39.3 %copy-start.14 = (bf16[1024]{0:T(1024)(128)(2,1)S(1)}, bf16[1024]{0:T(1024)(128)(2,1)}, u32[]{:S(2)}) copy-start(bf16[1024]{0:T(1024)(128)(2,1)} %param.17) | copy-start | bytes 6148
  12.9 39.3 %copy-start.15 = (s32[1,16,2]{1,2,0:T(2,128)S(1)}, s32[1,16,2]{1,2,0:T(2,128)}, u32[]{:S(2)}) copy-start(s32[1,16,2]{1,2,0:T(2,128)} %param.20) | copy-start | bytes 388
  13.6 29.0 %all-to-all-start.3 = ((f32[16,2,1024]{2,1,0:T(2,128)}), f32[16,2,1024]{2,1,0:T(2,128)S(1)}, u32[]{:S(2)}, u32[]{:S(2)}) async-start(f32[16,2,1024]{2,1,0:T(2,128)} %copy.74), calls=%async_computation.3 | async-start | bytes 262144 | tf_op jit(solution)/shard_map/all_to_all | solution.py:193
  21.0 144.0 %all-gather.5.cloned.1.call-start = ((), (), s32[]{:S(2)}) async-start(), calls=%async_computation.6 | async-start | bytes 1114112 | tf_op jit(solution)/shard_map/all_gather | solution.py:178
  43.3 16.3 %all-to-all-start = ((bf16[48,16,128]{2,0,1:T(8,128)(2,1)}), bf16[48,16,128]{2,0,1:T(8,128)(2,1)S(1)}, u32[]{:S(2)}, u32[]{:S(2)}) async-start(bf16[48,16,128]{2,0,1:T(8,128)(2,1)} %bitcast.106), calls=%async_computation | async-start | bytes 393216 | tf_op jit(solution)/shard_map/all_to_all | solution.py:145
  50.4 8.4 %copy-start.8 = (f32[16,2,1024]{2,1,0:T(2,128)S(1)}, f32[16,2,1024]{2,1,0:T(2,128)}, u32[]{:S(2)}) copy-start(f32[16,2,1024]{2,1,0:T(2,128)} %copy-done.7) | copy-start | bytes 393220
  98.3 8.4 %copy-start.6 = (bf16[48,1024]{0,1:T(8,128)(2,1)S(1)}, bf16[48,1024]{0,1:T(8,128)(2,1)}, u32[]{:S(2)}) copy-start(bf16[48,1024]{0,1:T(8,128)(2,1)} %get-tuple-element.25) | copy-start | bytes 294916
  98.3 9.2 %copy-start.5 = (bf16[48,1024]{0,1:T(8,128)(2,1)S(1)}, bf16[48,1024]{0,1:T(8,128)(2,1)}, u32[]{:S(2)}) copy-start(bf16[48,1024]{0,1:T(8,128)(2,1)} %get-tuple-element.28) | copy-start | bytes 294916
  99.1 12.4 %all-to-all-start.1 = ((bf16[96,8,128]{2,0,1:T(8,128)(2,1)}), bf16[96,8,128]{2,0,1:T(8,128)(2,1)}, u32[]{:S(2)}, u32[]{:S(2)}) async-start(bf16[96,8,128]{2,0,1:T(8,128)(2,1)} %copy.67), calls=%async_computation.1 | async-start | bytes 393216 | tf_op jit(solution)/shard_map/all_to_all | solution.py:127
  104.5 7.0 %copy-start.3 = (f32[128,1024]{1,0:T(8,128)S(1)}, f32[128,1024]{1,0:T(8,128)}, u32[]{:S(2)}) copy-start(f32[128,1024]{1,0:T(8,128)} %fusion.56) | copy-start | bytes 1572868
  115.4 23.5 %collective-permute-start.1 = (bf16[128,1024]{1,0:T(8,128)(2,1)S(1)}, bf16[128,1024]{1,0:T(8,128)(2,1)}, u32[]{:S(2)}, u32[]{:S(2)}) collective-permute-start(bf16[128,1024]{1,0:T(8,128)(2,1)S(1)} %fusion.13), channel_id=1, source_target_pairs={{0,4},{1,5},{4,8},{5,9},{8,12},{9,13},{12,14},{13,15},{14,10},{15,... | collective-permute-start | bytes 786440 | tf_op jit(solution)/shard_map/ppermute | solution.py:227
  115.6 21.9 %collective-permute-start.2 = (bf16[128,1024]{1,0:T(8,128)(2,1)S(1)}, bf16[128,1024]{1,0:T(8,128)(2,1)}, u32[]{:S(2)}, u32[]{:S(2)}) collective-permute-start(bf16[128,1024]{1,0:T(8,128)(2,1)S(1)} %fusion.13), channel_id=1, source_target_pairs={{4,0},{5,1},{8,4},{9,5},{12,8},{13,9},{14,12},{15,13},{10,14},{11,... | collective-permute-start | bytes 786440 | tf_op jit(solution)/shard_map/ppermute | solution.py:228
  118.2 12.0 %all-to-all-start.2 = ((bf16[16,2,1024]{2,1,0:T(2,128)(2,1)}), bf16[16,2,1024]{2,1,0:T(2,128)(2,1)S(1)}, u32[]{:S(2)}, u32[]{:S(2)}) async-start(bf16[16,2,1024]{2,1,0:T(2,128)(2,1)} %reshape.122), calls=%async_computation.2 | async-start | bytes 131072 | tf_op jit(solution)/shard_map/all_to_all | solution.py:170
  130.2 13.8 %all-to-all-start.4 = ((bf16[16,96,64]{1,2,0:T(8,128)(2,1)}), bf16[16,96,64]{1,2,0:T(8,128)(2,1)S(1)}, u32[]{:S(2)}, u32[]{:S(2)}) async-start(bf16[16,96,64]{1,2,0:T(8,128)(2,1)} %bitcast.31), calls=%async_computation.4 | async-start | bytes 524288 | tf_op jit(solution)/shard_map/all_to_all | solution.py:240
  134.5 5.9 %copy-start.12 = (bf16[192,1,128]{2,1,0:T(2,128)(2,1)S(1)}, bf16[192,1,128]{2,1,0:T(2,128)(2,1)}, u32[]{:S(2)}) copy-start(bf16[192,1,128]{2,1,0:T(2,128)(2,1)} %get-tuple-element.22) | copy-start | bytes 147460
  137.5 9.7 %collective-permute-start.4 = (bf16[128,1024]{1,0:T(8,128)(2,1)}, bf16[128,1024]{1,0:T(8,128)(2,1)}, u32[]{:S(2)}, u32[]{:S(2)}) collective-permute-start(bf16[128,1024]{1,0:T(8,128)(2,1)} %collective-permute-done.2), channel_id=1, source_target_pairs={{4,0},{5,1},{8,4},{9,5},{12,8},{13,9},{14,12},{15,13},{10,14},{11,... | collective-permute-start | bytes 786440 | tf_op jit(solution)/shard_map/ppermute | solution.py:228
  138.9 8.7 %collective-permute-start.3 = (bf16[128,1024]{1,0:T(8,128)(2,1)}, bf16[128,1024]{1,0:T(8,128)(2,1)}, u32[]{:S(2)}, u32[]{:S(2)}) collective-permute-start(bf16[128,1024]{1,0:T(8,128)(2,1)} %collective-permute-done.1), channel_id=1, source_target_pairs={{0,4},{1,5},{4,8},{5,9},{8,12},{9,13},{12,14},{13,15},{14,10},{15,... | collective-permute-start | bytes 786440 | tf_op jit(solution)/shard_map/ppermute | solution.py:227
  142.5 8.2 %copy-start.2 = (f32[192,1024]{1,0:T(8,128)S(1)}, f32[192,1024]{1,0:T(8,128)}, u32[]{:S(2)}) copy-start(f32[192,1024]{1,0:T(8,128)} %convolution_add_fusion.2) | copy-start | bytes 2359300
  147.2 9.5 %collective-permute-start.6 = (bf16[128,1024]{1,0:T(8,128)(2,1)}, bf16[128,1024]{1,0:T(8,128)(2,1)S(1)}, u32[]{:S(2)}, u32[]{:S(2)}) collective-permute-start(bf16[128,1024]{1,0:T(8,128)(2,1)} %collective-permute-done.4), channel_id=1, source_target_pairs={{4,0},{5,1},{8,4},{9,5},{12,8},{13,9},{14,12},{15,13},{10,14},{11,... | collective-permute-start | bytes 786440 | tf_op jit(solution)/shard_map/ppermute | solution.py:228
  147.6 6.9 %collective-permute-start.5 = (bf16[128,1024]{1,0:T(8,128)(2,1)}, bf16[128,1024]{1,0:T(8,128)(2,1)S(1)}, u32[]{:S(2)}, u32[]{:S(2)}) collective-permute-start(bf16[128,1024]{1,0:T(8,128)(2,1)} %collective-permute-done.3), channel_id=1, source_target_pairs={{0,4},{1,5},{4,8},{5,9},{8,12},{9,13},{12,14},{13,15},{14,10},{15,... | collective-permute-start | bytes 786440 | tf_op jit(solution)/shard_map/ppermute | solution.py:227
  149.4 7.8 %copy-start.10 = (bf16[192,1,128]{2,1,0:T(2,128)(2,1)S(1)}, bf16[192,1,128]{2,1,0:T(2,128)(2,1)}, u32[]{:S(2)}) copy-start(bf16[192,1,128]{2,1,0:T(2,128)(2,1)} %get-tuple-element.19) | copy-start | bytes 147460
  150.7 10.1 %copy-start.9 = (bf16[192,1,128]{2,1,0:T(2,128)(2,1)S(1)}, bf16[192,1,128]{2,1,0:T(2,128)(2,1)}, u32[]{:S(2)}) copy-start(bf16[192,1,128]{2,1,0:T(2,128)(2,1)} %get-tuple-element.18) | copy-start | bytes 147460
  150.8 10.4 %copy-start.11 = (bf16[192,1,128]{2,1,0:T(2,128)(2,1)S(1)}, bf16[192,1,128]{2,1,0:T(2,128)(2,1)}, u32[]{:S(2)}) copy-start(bf16[192,1,128]{2,1,0:T(2,128)(2,1)} %get-tuple-element.17) | copy-start | bytes 147460
  154.5 5.0 %collective-permute-start.7 = (bf16[64,1024]{1,0:T(8,128)(2,1)S(1)}, bf16[64,1024]{1,0:T(8,128)(2,1)S(1)}, u32[]{:S(2)}, u32[]{:S(2)}) collective-permute-start(bf16[64,1024]{1,0:T(8,128)(2,1)S(1)} %slice.59), channel_id=1, source_target_pairs={{0,4},{1,5},{4,8},{5,9},{8,12},{9,13},{12,14},{13,15},{14,10},{15,... | collective-permute-start | bytes 393224 | tf_op jit(solution)/shard_map/ppermute | solution.py:232
  156.7 4.2 %collective-permute-start.8 = (bf16[64,1024]{1,0:T(8,128)(2,1)S(1)}, bf16[64,1024]{1,0:T(8,128)(2,1)S(1)}, u32[]{:S(2)}, u32[]{:S(2)}) collective-permute-start(bf16[64,1024]{1,0:T(8,128)(2,1)S(1)} %slice.60), channel_id=1, source_target_pairs={{4,0},{5,1},{8,4},{9,5},{12,8},{13,9},{14,12},{15,13},{10,14},{11,... | collective-permute-start | bytes 393224 | tf_op jit(solution)/shard_map/ppermute | solution.py:233
  162.2 8.3 %collective-permute-start.9 = (f32[96,1024]{1,0:T(8,128)}, f32[96,1024]{1,0:T(8,128)}, u32[]{:S(2)}, u32[]{:S(2)}) collective-permute-start(f32[96,1024]{1,0:T(8,128)} %slice.62), channel_id=1, source_target_pairs={{0,1},{1,0},{2,3},{3,2},{4,5},{5,4},{6,7},{7,6},{8,9},{9,8},{10,11... | collective-permute-start | bytes 1179656 | tf_op jit(solution)/shard_map/ppermute | solution.py:235
  (2 other events, 3.3 us)
Sparse Core Ops, SparseCore 0:
  10.2 45.4 all-gather.2
  57.8 37.4 all-gather.4

commit v3 on v2

--- a/solution.py
+++ b/solution.py
@@ -202,10 +202,9 @@
     _, pull_back = jax.vjp(gelu_tanh, pre_one)
     grad_pre = pull_back(grad_hidden)[0].astype(jnp.bfloat16)
     order = list(range(0, pairs, 2)) + list(range(1, pairs, 2))[::-1]
-    spots = jnp.asarray(order, jnp.int32)
-    mine = jnp.asarray([order.index(p) for p in range(pairs)], jnp.int32)[
-        lax.axis_index("feat") // 2
-    ]
+    evens = (pairs + 1) // 2
+    pair = lax.axis_index("feat") // 2
+    mine = jnp.where(pair % 2 == 0, pair // 2, pairs - 1 - pair // 2)
     onward = [
         (2 * order[i] + c, 2 * order[(i + 1) % pairs] + c) for i in range(pairs) for c in range(2)
     ]
@@ -214,18 +213,23 @@
     left = jnp.transpose(left.reshape(4 * width, pairs, own_rows), (1, 0, 2))
 
     def term(hop, block):
-        owner = spots[lax.rem(mine + hop + pairs, pairs)]
+        spot = lax.rem(mine + hop + pairs, pairs)
+        owner = jnp.where(spot < evens, 2 * spot, 2 * (pairs - 1 - spot) + 1)
         return jnp.dot(
             lax.dynamic_index_in_dim(left, owner, 0, keepdims=False),
             block,
             preferred_element_type=jnp.float32,
         )
 
+    side_rows = jnp.concatenate([seed_hidden, sent_rows], axis=0)
+    side_rows = jnp.transpose(side_rows.reshape(own_seeds + slot_total, devices, -1), (1, 0, 2))
     total = term(0, grad_pre)
     going, coming = grad_pre, grad_pre
     for hop in range(1, (pairs + 1) // 2):
         going = lax.ppermute(going, "feat", onward)
         coming = lax.ppermute(coming, "feat", back)
+        if hop == 1:
+            side_rows, going, coming = lax.optimization_barrier((side_rows, going, coming))
         total = total + term(-hop, going) + term(hop, coming)
     if pairs % 2 == 0:
         cut = own_rows // 2
@@ -235,8 +239,6 @@
     from_other = lax.ppermute(total[: 2 * width], "feat", swap)
     both_one = total[2 * width :] + from_other
 
-    side_rows = jnp.concatenate([seed_hidden, sent_rows], axis=0)
-    side_rows = jnp.transpose(side_rows.reshape(own_seeds + slot_total, devices, -1), (1, 0, 2))
     side_rows = lax.all_to_all(side_rows, "feat", split_axis=0, concat_axis=0, tiled=True)
     slice_two = side_rows.shape[2]
     seed_cols = side_rows[:, :own_seeds].reshape(-1, slice_two)

time: 181 us -> 172 us (0.950)
  between operations: 34.7 us -> 14.4 us
  waiting for transfers between devices: 16.2 us -> 27.1 us
  starting transfers between devices: 40 us -> 37.7 us
  local copies, waits for them, and re-layouts: 20.8 us -> 22.7 us
    ppermute x3, waiting for transfers between devices: 2.44 us -> 10.1 us  [shards(): going = lax.ppermute(going, 'feat', onward)]
    all_to_all x1, waiting for transfers between devices: 0.01 us -> 3.89 us  [shards(): lax.all_to_all(slot_grads.reshape(devices, slots_peer, hidden_width), 'fe...]
    all_to_all x1, waiting for transfers between devices: 0.01 us -> 3.35 us  [shards(): lax.all_to_all(self_all, 'feat', split_axis=1, concat_axis=0, tiled=True)]
    ppermute x3, waiting for transfers between devices: 2.69 us -> 0.01 us  [shards(): coming = lax.ppermute(coming, 'feat', back)]
    all_to_all x1, starting transfers between devices: 6.02 us -> 3.78 us  [shards(): lax.all_to_all(self_all, 'feat', split_axis=1, concat_axis=0, tiled=True)]
    ppermute x1, waiting for transfers between devices: 2.01 us -> 0.11 us  [shards(): first = lax.ppermute(going[:cut], 'feat', onward)]
    ppermute x3, starting transfers between devices: 2.15 us -> 4.04 us  [shards(): going = lax.ppermute(going, 'feat', onward)]
  transfers between devices with their start and end apart: 17 -> 17, of which waited for: 7 -> 8; matrix products, arithmetic and copies ran while one was open for 29% -> 31% of each run, Pallas kernels for 19% -> 20%
where the time goes in v3:
time: 172 us; the launch traced here: 171 us
  starting transfers between devices  37.7 us (22%)
  Pallas kernels  34.1 us (20%)
  matrix products  29.6 us (17%)
  waiting for transfers between devices  27.1 us (16%)
  local copies, waits for them, and re-layouts  22.7 us (13%)
  between operations  14.4 us (8%)
  other arithmetic  5.12 us (3%)
    pallas_call x1, Pallas kernels, gather_sum(): pl.pallas_call(add_rows, grid=(targets // step_rows,), out_shape=jax.Shap...  34.1 us
    ppermute x3, waiting for transfers between devices, shards(): going = lax.ppermute(going, 'feat', onward)  10.1 us
    dot_general x4, matrix products, contract_lead(): lax.dot_general(left_side, right_side, (((0,), (0,)), ((), ())), preferre...  9.85 us
    dot_general x8, matrix products, term(): jnp.dot(lax.dynamic_index_in_dim(left, owner, 0, keepdims=False), block,...  9.72 us
    all_to_all x1, starting transfers between devices, shards(): lax.all_to_all(slot_grads.reshape(devices, slots_peer, hidden_width), 'fe...  7.32 us
    all_to_all x1, starting transfers between devices, to_blocks(): lax.all_to_all(columns, 'feat', split_axis=1, concat_axis=0, axis_index_g...  5.84 us
    all_to_all x1, starting transfers between devices, shards(): lax.all_to_all(outgoing, 'feat', split_axis=0, concat_axis=0, tiled=True)  5.34 us
    all_to_all x1, starting transfers between devices, shards(): lax.all_to_all(side_rows, 'feat', split_axis=0, concat_axis=0, tiled=True)  4.42 us
  transfers between devices with their start and end apart: 17, of which 8 were waited for; matrix products, arithmetic and copies ran while one was open for 31% of the time, Pallas kernels for 20%

profile of v3, /device:TPU:1, one launch (start us, length us, event | category | flops | bytes accessed | tf_op | source)
XLA Modules:
  0.0 170.7 jit_solution(10290838822655981458)
XLA Ops:
  10.0 2.4 %fusion.5 = f32[64,1024,1]{1,0,2:T(8,128)S(1)} fusion(bf16[64,1024]{1,0:T(8,128)(2,1)} %param.21, bf16[1024,1024]{1,0:T(8,128)(2,1)} %param.17, f32[64]{0:T(128)S(1)} %convert_element_type.50), kind=kOutput, calls=%fused_computation.11 | convolution fusion | flops 134283264 | bytes 2490624 | tf_op jit(solution)/shard_map/dot_general | solution.py:22
  13.5 7.3 %all-to-all-start.3 = ((f32[16,2,1024]{2,1,0:T(2,128)}), f32[16,2,1024]{2,1,0:T(2,128)S(1)}, u32[]{:S(2)}, u32[]{:S(2)}) async-start(f32[16,2,1024]{2,1,0:T(2,128)} %copy.72), calls=%async_computation.3 | async-start | bytes 262144 | tf_op jit(solution)/shard_map/all_to_all | solution.py:193
  21.9 1.7 fusion.54
  23.7 1.8 %reshape.104 = s32[25,8,2,128]{3,2,1,0:T(2,128)} reshape(s32[25,2048]{1,0:T(8,128)} %bitcast.108) | data formatting | bytes 409600 | tf_op jit(solution)/shard_map/reshape | solution.py:137
  26.2 3.9 %all-to-all-done.3 = f32[16,2,1024]{2,1,0:T(2,128)S(1)} async-done(((f32[16,2,1024]{2,1,0:T(2,128)}), f32[16,2,1024]{2,1,0:T(2,128)S(1)}, u32[]{:S(2)}, u32[]{:S(2)}) %all-to-all-start.3) | async-done | bytes 131104 | tf_op jit(solution)/shard_map/all_to_all | solution.py:193
  30.8 3.8 %all-to-all-start = ((bf16[48,16,128]{2,0,1:T(8,128)(2,1)}), bf16[48,16,128]{2,0,1:T(8,128)(2,1)S(1)}, u32[]{:S(2)}, u32[]{:S(2)}) async-start(bf16[48,16,128]{2,0,1:T(8,128)(2,1)} %bitcast.90), calls=%async_computation | async-start | bytes 393216 | tf_op jit(solution)/shard_map/all_to_all | solution.py:145
  35.7 1.8 %reshape.109 = bf16[48,8,2,128]{3,2,1,0:T(2,128)(2,1)} reshape(bf16[48,2048]{1,0:T(8,128)(2,1)} %get-tuple-element.19) | data formatting | bytes 393216 | tf_op jit(solution)/shard_map/reshape | solution.py:137
  37.4 1.5 fusion.58
  39.6 3.4 %all-to-all-done = bf16[48,16,128]{2,0,1:T(8,128)(2,1)S(1)} async-done(((bf16[48,16,128]{2,0,1:T(8,128)(2,1)}), bf16[48,16,128]{2,0,1:T(8,128)(2,1)S(1)}, u32[]{:S(2)}, u32[]{:S(2)}) %all-to-all-start) | async-done | bytes 196640 | tf_op jit(solution)/shard_map/all_to_all | solution.py:145
  43.0 2.7 %fusion.57 = f32[128,1024]{1,0:T(8,128)} fusion(bf16[768,128]{1,0:T(8,128)(2,1)S(1)} %bitcast.99, bf16[768,1024]{1,0:T(8,128)(2,1)} %param.13), kind=kOutput, calls=%fused_computation.96 | convolution fusion | flops 201326592 | bytes 2293760 | tf_op jit(solution)/shard_map/dot_general | solution.py:16
  45.7 34.1 %gather_sum.1 = f32[1024,128]{1,0:T(8,128)S(1)} custom-call(s32[25,1024]{1,0:T(8,128)S(1)} %bitcast.94, bf16[48,8192]{1,0:T(8,128)(2,1)S(1)} %copy-done.1, bf16[48,8192]{1,0:T(8,128)(2,1)S(1)} %collective-permute-done.partner_ref), custom_call_target="tpu_custom_call" | custom-call | flops 3276800 | bytes 104857600 | tf_op jit(solution)/shard_map/gather_sum/pallas_call | solution.py:72
  82.5 5.8 %all-to-all-start.1 = ((bf16[96,8,128]{2,0,1:T(8,128)(2,1)}), bf16[96,8,128]{2,0,1:T(8,128)(2,1)S(1)}, u32[]{:S(2)}, u32[]{:S(2)}) async-start(bf16[96,8,128]{2,0,1:T(8,128)(2,1)} %copy.65), calls=%async_computation.1 | async-start | bytes 393216 | tf_op jit(solution)/shard_map/all_to_all | solution.py:127
  88.3 1.4 constant_dynamic-slice_fusion.8
  91.7 1.6 constant_dynamic-slice_fusion.2
  93.3 3.0 %all-to-all-done.1 = bf16[96,8,128]{2,0,1:T(8,128)(2,1)S(1)} async-done(((bf16[96,8,128]{2,0,1:T(8,128)(2,1)}), bf16[96,8,128]{2,0,1:T(8,128)(2,1)S(1)}, u32[]{:S(2)}, u32[]{:S(2)}) %all-to-all-start.1) | async-done | bytes 196640 | tf_op jit(solution)/shard_map/all_to_all | solution.py:127
  96.3 2.1 %multiply_convert_fusion = (bf16[128,1024]{1,0:T(8,128)(2,1)S(1)}, f32[128,1024]{1,0:T(8,128)S(1)}) fusion(f32[1024]{0:T(1024)S(1)} %convert_element_type.43, f32[128,1024]{1,0:T(8,128)} %fusion.57, bf16[768,128]{1,0:T(8,128)(2,1)S(1)} %bitcast.100, bf16[768,1024]{1,0:T(8,128)(2,1)} %param.14), kind=kOutput, calls=%fused_computation.29 | convolution fusion | flops 202768384 | bytes 3084288 | tf_op jit(solution)/shard_map/dot_general | solution.py:16
  99.4 1.5 fusion.14
  103.0 5.3 %all-to-all-start.2 = ((bf16[16,2,1024]{2,1,0:T(2,128)(2,1)}), bf16[16,2,1024]{2,1,0:T(2,128)(2,1)}, u32[]{:S(2)}, u32[]{:S(2)}) async-start(bf16[16,2,1024]{2,1,0:T(2,128)(2,1)} %reshape.106), calls=%async_computation.2 | async-start | bytes 131072 | tf_op jit(solution)/shard_map/all_to_all | solution.py:170
  110.5 4.1 %all-to-all-done.2 = bf16[16,2,1024]{2,1,0:T(2,128)(2,1)} async-done(((bf16[16,2,1024]{2,1,0:T(2,128)(2,1)}), bf16[16,2,1024]{2,1,0:T(2,128)(2,1)}, u32[]{:S(2)}, u32[]{:S(2)}) %all-to-all-start.2) | async-done | bytes 65568 | tf_op jit(solution)/shard_map/all_to_all | solution.py:170
  115.4 2.9 %fusion.6 = bf16[64,1024]{1,0:T(8,128)(2,1)} fusion(f32[64,1024]{1,0:T(8,128)S(1)} %fusion.52, bf16[1024,1024]{1,0:T(8,128)(2,1)} %param.17, bf16[32,1024]{1,0:T(8,128)(2,1)S(1)} %reshape.107, f32[64]{0:T(128)S(1)} %convert_element_type.50, f32[64,32]{0,1:T(8,128)S(1)} %convert_reduce_fusion), kind=kOutput, calls=%fused_computation.14 | convolution fusion | flops 138676224 | bytes 2564352 | tf_op jit(solution)/shard_map/dot_general | solution.py:186
  118.3 4.4 %all-to-all-start.4 = ((bf16[16,96,64]{1,2,0:T(8,128)(2,1)}), bf16[16,96,64]{1,2,0:T(8,128)(2,1)S(1)}, u32[]{:S(2)}, u32[]{:S(2)}) async-start(bf16[16,96,64]{1,2,0:T(8,128)(2,1)} %bitcast.15), calls=%async_computation.4 | async-start | bytes 524288 | tf_op jit(solution)/shard_map/all_to_all | solution.py:242
  122.7 1.5 collective-permute-start.3
  124.3 1.3 convolution_add_fusion.2
  125.5 8.1 %collective-permute-done.3 = bf16[128,1024]{1,0:T(8,128)(2,1)} collective-permute-done((bf16[128,1024]{1,0:T(8,128)(2,1)}, bf16[128,1024]{1,0:T(8,128)(2,1)}, u32[]{:S(2)}, u32[]{:S(2)}) %collective-permute-start.3) | collective-permute-done | bytes 262176 | tf_op jit(solution)/shard_map/ppermute | solution.py:229
  133.6 2.3 %collective-permute-start.5 = (bf16[128,1024]{1,0:T(8,128)(2,1)}, bf16[128,1024]{1,0:T(8,128)(2,1)}, u32[]{:S(2)}, u32[]{:S(2)}) collective-permute-start(bf16[128,1024]{1,0:T(8,128)(2,1)} %collective-permute-done.3), channel_id=1, source_target_pairs={{0,4},{1,5},{4,8},{5,9},{8,12},{9,13},{12,14},{13,15},{14,10},{15,... | collective-permute-start | bytes 786440 | tf_op jit(solution)/shard_map/ppermute | solution.py:229
  140.4 2.0 %collective-permute-done.5 = bf16[128,1024]{1,0:T(8,128)(2,1)} collective-permute-done((bf16[128,1024]{1,0:T(8,128)(2,1)}, bf16[128,1024]{1,0:T(8,128)(2,1)}, u32[]{:S(2)}, u32[]{:S(2)}) %collective-permute-start.5) | collective-permute-done | bytes 262176 | tf_op jit(solution)/shard_map/ppermute | solution.py:229
  145.3 1.7 collective-permute-start.8
  146.9 1.2 fusion.25
  148.3 1.8 %collective-permute-done.8 = bf16[64,1024]{1,0:T(8,128)(2,1)S(1)} collective-permute-done((bf16[64,1024]{1,0:T(8,128)(2,1)S(1)}, bf16[64,1024]{1,0:T(8,128)(2,1)S(1)}, u32[]{:S(2)}, u32[]{:S(2)}) %collective-permute-start.8) | collective-permute-done | bytes 131104 | tf_op jit(solution)/shard_map/ppermute | solution.py:237
  154.2 2.4 %collective-permute-start.9 = (f32[96,1024]{1,0:T(8,128)}, f32[96,1024]{1,0:T(8,128)}, u32[]{:S(2)}, u32[]{:S(2)}) collective-permute-start(f32[96,1024]{1,0:T(8,128)} %slice.62), channel_id=1, source_target_pairs={{0,1},{1,0},{2,3},{3,2},{4,5},{5,4},{6,7},{7,6},{8,9},{9,8},{10,11... | collective-permute-start | bytes 1179656 | tf_op jit(solution)/shard_map/ppermute | solution.py:239
  156.6 2.3 %fusion.60 = f32[64,1024]{1,0:T(8,128)} fusion(bf16[512,64]{1,0:T(8,128)(2,1)S(1)} %bitcast.103, bf16[512,1024]{1,0:T(8,128)(2,1)} %all-gather.5.cloned.1.call-done), kind=kOutput, calls=%fused_computation.99 | convolution fusion | flops 67108864 | bytes 1376256 | tf_op jit(solution)/shard_map/dot_general | solution.py:16
  159.3 2.8 %fusion.59 = f32[64,1024]{1,0:T(8,128)} fusion(bf16[1024,64]{0,1:T(8,128)(2,1)S(1)} %reshape.112, bf16[1024,1024]{1,0:T(8,128)(2,1)} %all-gather.3.cloned.1.call-done), kind=kOutput, calls=%fused_computation.98 | convolution fusion | flops 134217728 | bytes 2490368 | tf_op jit(solution)/shard_map/dot_general | solution.py:16
  (100 shorter events, 32.5 us)
Async XLA Ops:
  7.2 30.3 %copy-start = (bf16[1024,1024]{1,0:T(8,128)(2,1)S(1)}, bf16[1024,1024]{1,0:T(8,128)(2,1)}, u32[]{:S(2)}) copy-start(bf16[1024,1024]{1,0:T(8,128)(2,1)} %param.16) | copy-start | bytes 6291460
  7.2 13.9 %copy-start.4 = (bf16[64,1024]{1,0:T(8,128)(2,1)S(1)}, bf16[64,1024]{1,0:T(8,128)(2,1)}, u32[]{:S(2)}) copy-start(bf16[64,1024]{1,0:T(8,128)(2,1)} %param.21) | copy-start | bytes 393220
  7.2 73.5 %all-gather.3.cloned.1.call-start = ((), (), s32[]{:S(2)}) async-start(), calls=%async_computation.5 | async-start | bytes 2228224 | tf_op jit(solution)/shard_map/all_gather | solution.py:140
  10.0 13.5 %copy-start.14 = (bf16[1024]{0:T(1024)(128)(2,1)S(1)}, bf16[1024]{0:T(1024)(128)(2,1)}, u32[]{:S(2)}) copy-start(bf16[1024]{0:T(1024)(128)(2,1)} %param.15) | copy-start | bytes 6148
  10.0 13.5 %copy-start.15 = (s32[1,16,2]{1,2,0:T(2,128)S(1)}, s32[1,16,2]{1,2,0:T(2,128)}, u32[]{:S(2)}) copy-start(s32[1,16,2]{1,2,0:T(2,128)} %param.18) | copy-start | bytes 388
  13.5 16.6 %all-to-all-start.3 = ((f32[16,2,1024]{2,1,0:T(2,128)}), f32[16,2,1024]{2,1,0:T(2,128)S(1)}, u32[]{:S(2)}, u32[]{:S(2)}) async-start(f32[16,2,1024]{2,1,0:T(2,128)} %copy.72), calls=%async_computation.3 | async-start | bytes 262144 | tf_op jit(solution)/shard_map/all_to_all | solution.py:193
  20.8 135.8 %all-gather.5.cloned.1.call-start = ((), (), s32[]{:S(2)}) async-start(), calls=%async_computation.6 | async-start | bytes 1114112 | tf_op jit(solution)/shard_map/all_gather | solution.py:178
  20.9 24.8 %collective-permute-start = (bf16[48,8192]{1,0:T(8,128)(2,1)}, bf16[48,8192]{1,0:T(8,128)(2,1)S(1)}, u32[]{:S(2)}, u32[]{:S(2)}) collective-permute-start(bf16[48,8192]{1,0:T(8,128)(2,1)} %own_ref), channel_id=1, source_target_pairs={{0,1},{1,0},{2,3},{3,2},{4,5},{5,4},{6,7},{7,6},{8,9},{9,8},{10,11... | collective-permute-start | bytes 2359304 | tf_op jit(solution)/shard_map/ppermute | solution.py:143
  30.8 12.2 %all-to-all-start = ((bf16[48,16,128]{2,0,1:T(8,128)(2,1)}), bf16[48,16,128]{2,0,1:T(8,128)(2,1)S(1)}, u32[]{:S(2)}, u32[]{:S(2)}) async-start(bf16[48,16,128]{2,0,1:T(8,128)(2,1)} %bitcast.90), calls=%async_computation | async-start | bytes 393216 | tf_op jit(solution)/shard_map/all_to_all | solution.py:145
  35.6 3.2 %copy-start.7 = (f32[16,2,1024]{2,1,0:T(2,128)S(1)}, f32[16,2,1024]{2,1,0:T(2,128)}, u32[]{:S(2)}) copy-start(f32[16,2,1024]{2,1,0:T(2,128)} %copy-done.6) | copy-start | bytes 393220
  43.0 2.7 %copy-start.1 = (bf16[48,8192]{1,0:T(8,128)(2,1)S(1)}, bf16[48,8192]{1,0:T(8,128)(2,1)}, u32[]{:S(2)}) copy-start(bf16[48,8192]{1,0:T(8,128)(2,1)} %own_ref) | copy-start | bytes 2359300
  81.5 8.9 %copy-start.5 = (bf16[48,1024]{0,1:T(8,128)(2,1)S(1)}, bf16[48,1024]{0,1:T(8,128)(2,1)}, u32[]{:S(2)}) copy-start(bf16[48,1024]{0,1:T(8,128)(2,1)} %get-tuple-element.31) | copy-start | bytes 294916
  82.5 13.8 %all-to-all-start.1 = ((bf16[96,8,128]{2,0,1:T(8,128)(2,1)}), bf16[96,8,128]{2,0,1:T(8,128)(2,1)S(1)}, u32[]{:S(2)}, u32[]{:S(2)}) async-start(bf16[96,8,128]{2,0,1:T(8,128)(2,1)} %copy.65), calls=%async_computation.1 | async-start | bytes 393216 | tf_op jit(solution)/shard_map/all_to_all | solution.py:127
  98.4 1.0 copy-start.8
  98.4 1.0 copy-start.13
  100.9 17.5 %collective-permute-start.2 = (bf16[128,1024]{1,0:T(8,128)(2,1)}, bf16[128,1024]{1,0:T(8,128)(2,1)}, u32[]{:S(2)}, u32[]{:S(2)}) collective-permute-start(bf16[128,1024]{1,0:T(8,128)(2,1)} %fusion.14), channel_id=1, source_target_pairs={{4,0},{5,1},{8,4},{9,5},{12,8},{13,9},{14,12},{15,13},{10,14},{11,... | collective-permute-start | bytes 786440 | tf_op jit(solution)/shard_map/ppermute | solution.py:230
  102.0 16.3 %collective-permute-start.1 = (bf16[128,1024]{1,0:T(8,128)(2,1)}, bf16[128,1024]{1,0:T(8,128)(2,1)}, u32[]{:S(2)}, u32[]{:S(2)}) collective-permute-start(bf16[128,1024]{1,0:T(8,128)(2,1)} %fusion.14), channel_id=1, source_target_pairs={{0,4},{1,5},{4,8},{5,9},{8,12},{9,13},{12,14},{13,15},{14,10},{15,... | collective-permute-start | bytes 786440 | tf_op jit(solution)/shard_map/ppermute | solution.py:229
  103.0 11.6 %all-to-all-start.2 = ((bf16[16,2,1024]{2,1,0:T(2,128)(2,1)}), bf16[16,2,1024]{2,1,0:T(2,128)(2,1)}, u32[]{:S(2)}, u32[]{:S(2)}) async-start(bf16[16,2,1024]{2,1,0:T(2,128)(2,1)} %reshape.106), calls=%async_computation.2 | async-start | bytes 131072 | tf_op jit(solution)/shard_map/all_to_all | solution.py:170
  118.3 18.0 %copy-start.10 = (bf16[192,1,128]{2,1,0:T(2,128)(2,1)S(1)}, bf16[192,1,128]{2,1,0:T(2,128)(2,1)}, u32[]{:S(2)}) copy-start(bf16[192,1,128]{2,1,0:T(2,128)(2,1)} %get-tuple-element.26) | copy-start | bytes 147460
  118.3 19.2 %copy-start.9 = (bf16[192,1,128]{2,1,0:T(2,128)(2,1)S(1)}, bf16[192,1,128]{2,1,0:T(2,128)(2,1)}, u32[]{:S(2)}) copy-start(bf16[192,1,128]{2,1,0:T(2,128)(2,1)} %get-tuple-element.27) | copy-start | bytes 147460
  118.3 21.6 %all-to-all-start.4 = ((bf16[16,96,64]{1,2,0:T(8,128)(2,1)}), bf16[16,96,64]{1,2,0:T(8,128)(2,1)S(1)}, u32[]{:S(2)}, u32[]{:S(2)}) async-start(bf16[16,96,64]{1,2,0:T(8,128)(2,1)} %bitcast.15), calls=%async_computation.4 | async-start | bytes 524288 | tf_op jit(solution)/shard_map/all_to_all | solution.py:242
  122.7 16.0 %copy-start.12 = (bf16[192,1,128]{2,1,0:T(2,128)(2,1)S(1)}, bf16[192,1,128]{2,1,0:T(2,128)(2,1)}, u32[]{:S(2)}) copy-start(bf16[192,1,128]{2,1,0:T(2,128)(2,1)} %get-tuple-element.28) | copy-start | bytes 147460
  122.7 10.9 %collective-permute-start.3 = (bf16[128,1024]{1,0:T(8,128)(2,1)}, bf16[128,1024]{1,0:T(8,128)(2,1)}, u32[]{:S(2)}, u32[]{:S(2)}) collective-permute-start(bf16[128,1024]{1,0:T(8,128)(2,1)} %collective-permute-done.1), channel_id=1, source_target_pairs={{0,4},{1,5},{4,8},{5,9},{8,12},{9,13},{12,14},{13,15},{14,10},{15,... | collective-permute-start | bytes 786440 | tf_op jit(solution)/shard_map/ppermute | solution.py:229
  124.2 11.7 %collective-permute-start.4 = (bf16[128,1024]{1,0:T(8,128)(2,1)}, bf16[128,1024]{1,0:T(8,128)(2,1)}, u32[]{:S(2)}, u32[]{:S(2)}) collective-permute-start(bf16[128,1024]{1,0:T(8,128)(2,1)} %collective-permute-done.2), channel_id=1, source_target_pairs={{4,0},{5,1},{8,4},{9,5},{12,8},{13,9},{14,12},{15,13},{10,14},{11,... | collective-permute-start | bytes 786440 | tf_op jit(solution)/shard_map/ppermute | solution.py:230
  133.6 8.7 %collective-permute-start.5 = (bf16[128,1024]{1,0:T(8,128)(2,1)}, bf16[128,1024]{1,0:T(8,128)(2,1)}, u32[]{:S(2)}, u32[]{:S(2)}) collective-permute-start(bf16[128,1024]{1,0:T(8,128)(2,1)} %collective-permute-done.3), channel_id=1, source_target_pairs={{0,4},{1,5},{4,8},{5,9},{8,12},{9,13},{12,14},{13,15},{14,10},{15,... | collective-permute-start | bytes 786440 | tf_op jit(solution)/shard_map/ppermute | solution.py:229
  135.9 8.4 %collective-permute-start.6 = (bf16[128,1024]{1,0:T(8,128)(2,1)}, bf16[128,1024]{1,0:T(8,128)(2,1)}, u32[]{:S(2)}, u32[]{:S(2)}) collective-permute-start(bf16[128,1024]{1,0:T(8,128)(2,1)} %collective-permute-done.4), channel_id=1, source_target_pairs={{4,0},{5,1},{8,4},{9,5},{12,8},{13,9},{14,12},{15,13},{10,14},{11,... | collective-permute-start | bytes 786440 | tf_op jit(solution)/shard_map/ppermute | solution.py:230
  140.3 11.0 %copy-start.11 = (bf16[192,1,128]{2,1,0:T(2,128)(2,1)S(1)}, bf16[192,1,128]{2,1,0:T(2,128)(2,1)}, u32[]{:S(2)}) copy-start(bf16[192,1,128]{2,1,0:T(2,128)(2,1)} %get-tuple-element.23) | copy-start | bytes 147460
  143.3 5.0 %collective-permute-start.7 = (bf16[64,1024]{1,0:T(8,128)(2,1)S(1)}, bf16[64,1024]{1,0:T(8,128)(2,1)S(1)}, u32[]{:S(2)}, u32[]{:S(2)}) collective-permute-start(bf16[64,1024]{1,0:T(8,128)(2,1)S(1)} %slice.59), channel_id=1, source_target_pairs={{0,4},{1,5},{4,8},{5,9},{8,12},{9,13},{12,14},{13,15},{14,10},{15,... | collective-permute-start | bytes 393224 | tf_op jit(solution)/shard_map/ppermute | solution.py:236
  145.3 4.9 %collective-permute-start.8 = (bf16[64,1024]{1,0:T(8,128)(2,1)S(1)}, bf16[64,1024]{1,0:T(8,128)(2,1)S(1)}, u32[]{:S(2)}, u32[]{:S(2)}) collective-permute-start(bf16[64,1024]{1,0:T(8,128)(2,1)S(1)} %slice.60), channel_id=1, source_target_pairs={{4,0},{5,1},{8,4},{9,5},{12,8},{13,9},{14,12},{15,13},{10,14},{11,... | collective-permute-start | bytes 393224 | tf_op jit(solution)/shard_map/ppermute | solution.py:237
  152.5 0.9 copy-start.2
  154.2 7.9 %collective-permute-start.9 = (f32[96,1024]{1,0:T(8,128)}, f32[96,1024]{1,0:T(8,128)}, u32[]{:S(2)}, u32[]{:S(2)}) collective-permute-start(f32[96,1024]{1,0:T(8,128)} %slice.62), channel_id=1, source_target_pairs={{0,1},{1,0},{2,3},{3,2},{4,5},{5,4},{6,7},{7,6},{8,9},{9,8},{10,11... | collective-permute-start | bytes 1179656 | tf_op jit(solution)/shard_map/ppermute | solution.py:239
  156.6 5.5 %copy-start.3 = (f32[192,1024]{1,0:T(8,128)S(1)}, f32[192,1024]{1,0:T(8,128)}, u32[]{:S(2)}) copy-start(f32[192,1024]{1,0:T(8,128)} %copy-done.2) | copy-start | bytes 2359300
  (1 other events, 0.7 us)
Sparse Core Ops, SparseCore 0:
  10.2 45.1 all-gather.2
  57.5 37.1 all-gather.4

commit v4 on v3

--- a/solution.py
+++ b/solution.py
@@ -142,10 +142,32 @@
     features = jnp.pad(node_features, ((0, spare), (0, 0)))
     partner = lax.ppermute(features, "feat", swap)
     self_all = node_features[:, :targets]
-    self_cols = lax.all_to_all(self_all, "feat", split_axis=1, concat_axis=0, tiled=True)
+    peer_rows = send_rows[0]
+    slots_peer = peer_rows.shape[1]
+    slot_total = devices * slots_peer
+    fanout_two = neighbors_two.shape[1]
+    keep_mask = jnp.arange(fanout_two, dtype=jnp.int32)[None, :] < degree_two[:, None]
+    slot_ids = jnp.arange(slot_total, dtype=jnp.int32)
+    slot_hits = (neighbors_two[:, :, None] == slot_ids[None, None, :]) & keep_mask[:, :, None]
+    ref_count = jnp.sum(slot_hits.astype(jnp.float32), axis=1)
+    degree_float = degree_two.astype(jnp.float32)[:, None]
+    back_self = contract_last(out_grad, weight_self_two)
+    per_neighbor = contract_last(out_grad, weight_neigh_two) / degree_float
+    slot_grads = exact_lead(ref_count, per_neighbor)
+    blocks = jnp.transpose(self_all.reshape(width, devices, own_rows), (1, 0, 2))
+    slot_grads = slot_grads.astype(jnp.bfloat16).reshape(devices, -1, own_rows)
+    swapped = lax.all_to_all(
+        jnp.concatenate([blocks, slot_grads], axis=1),
+        "feat",
+        split_axis=0,
+        concat_axis=0,
+        tiled=True,
+    )
     self_own = my_targets(self_all)
     self_other = my_targets(partner[:width, :targets])
-    features, self_cols = lax.optimization_barrier((features, self_cols))
+    features, swapped = lax.optimization_barrier((features, swapped))
+    self_cols = swapped[:, :width].reshape(devices * width, own_rows)
+    returned = swapped[:, width:].reshape(slot_total, hidden_width)
     summed_one = gather_sum(features, partner, my_targets(neighbors_one.T))
     mean_pair = (summed_one[:, : 2 * (width + spare)] / fanout_one).astype(jnp.bfloat16).T
     mean_pair, all_out_grad = lax.optimization_barrier((mean_pair, all_out_grad))
@@ -157,47 +179,17 @@
         + bias_one.astype(jnp.float32)
     )
     hidden_one = gelu_tanh(pre_one).astype(jnp.bfloat16)
-    peer_rows = send_rows[0]
-    slots_peer = peer_rows.shape[1]
-    slot_total = devices * slots_peer
     row_hits = (
         peer_rows.reshape(-1)[:, None] == jnp.arange(own_rows, dtype=jnp.int32)[None, :]
-    ).astype(jnp.float32)
-    sent_rows = jnp.dot(
-        row_hits.astype(jnp.bfloat16), hidden_one, preferred_element_type=jnp.float32
     ).astype(jnp.bfloat16)
+    sent_rows = jnp.dot(row_hits, hidden_one, preferred_element_type=jnp.float32).astype(
+        jnp.bfloat16
+    )
     outgoing = sent_rows.reshape(devices, slots_peer, hidden_width)
-    incoming = lax.all_to_all(outgoing, "feat", split_axis=0, concat_axis=0, tiled=True)
-    fanout_two = neighbors_two.shape[1]
-    keep_mask = jnp.arange(fanout_two, dtype=jnp.int32)[None, :] < degree_two[:, None]
-    slot_ids = jnp.arange(slot_total, dtype=jnp.int32)
-    slot_hits = (neighbors_two[:, :, None] == slot_ids[None, None, :]) & keep_mask[:, :, None]
-    ref_count = jnp.sum(slot_hits.astype(jnp.float32), axis=1)
-    degree_float = degree_two.astype(jnp.float32)[:, None]
     slot_out = exact_lead(ref_count / degree_float, out_grad.astype(jnp.float32))
     all_slot_out = lax.all_gather(slot_out.astype(jnp.bfloat16), "feat", axis=0, tiled=True)
-    summed_two = jnp.dot(
-        ref_count.astype(jnp.bfloat16),
-        incoming.reshape(slot_total, hidden_width),
-        preferred_element_type=jnp.float32,
-    )
-    mean_two = (summed_two / degree_float).astype(jnp.bfloat16)
     seed_hidden = hidden_one[:own_seeds]
-    out_full = jnp.dot(seed_hidden, weight_self_two, preferred_element_type=jnp.float32) + jnp.dot(
-        mean_two, weight_neigh_two, preferred_element_type=jnp.float32
-    )
-    layer_out = out_full.astype(jnp.bfloat16)
-    back_self = contract_last(out_grad, weight_self_two)
-    per_neighbor = contract_last(out_grad, weight_neigh_two) / degree_float
-    slot_grads = exact_lead(ref_count, per_neighbor)
-    returned = lax.all_to_all(
-        slot_grads.reshape(devices, slots_peer, hidden_width),
-        "feat",
-        split_axis=0,
-        concat_axis=0,
-        tiled=True,
-    )
-    grad_hidden = exact_lead(row_hits, returned.reshape(slot_total, hidden_width))
+    grad_hidden = contract_lead(row_hits, returned)
     grad_hidden = grad_hidden + jnp.pad(back_self, ((0, own_rows - own_seeds), (0, 0)))
     _, pull_back = jax.vjp(gelu_tanh, pre_one)
     grad_pre = pull_back(grad_hidden)[0].astype(jnp.bfloat16)
@@ -229,6 +221,8 @@
         going = lax.ppermute(going, "feat", onward)
         coming = lax.ppermute(coming, "feat", back)
         if hop == 1:
+            outgoing, going, coming = lax.optimization_barrier((outgoing, going, coming))
+        if hop == 2:
             side_rows, going, coming = lax.optimization_barrier((side_rows, going, coming))
         total = total + term(-hop, going) + term(hop, coming)
     if pairs % 2 == 0:
@@ -238,6 +232,18 @@
         total = total + term(pairs // 2, jnp.concatenate([first, second], axis=0))
     from_other = lax.ppermute(total[: 2 * width], "feat", swap)
     both_one = total[2 * width :] + from_other
+
+    incoming = lax.all_to_all(outgoing, "feat", split_axis=0, concat_axis=0, tiled=True)
+    summed_two = jnp.dot(
+        ref_count.astype(jnp.bfloat16),
+        incoming.reshape(slot_total, hidden_width),
+        preferred_element_type=jnp.float32,
+    )
+    mean_two = (summed_two / degree_float).astype(jnp.bfloat16)
+    out_full = jnp.dot(seed_hidden, weight_self_two, preferred_element_type=jnp.float32) + jnp.dot(
+        mean_two, weight_neigh_two, preferred_element_type=jnp.float32
+    )
+    layer_out = out_full.astype(jnp.bfloat16)
 
     side_rows = lax.all_to_all(side_rows, "feat", split_axis=0, concat_axis=0, tiled=True)
     slice_two = side_rows.shape[2]

time: 172 us -> 164 us (0.953)
  waiting for transfers between devices: 27.1 us -> 21.5 us
  starting transfers between devices: 37.7 us -> 33.8 us
  matrix products: 29.6 us -> 33.2 us
  local copies, waits for them, and re-layouts: 22.7 us -> 19.6 us
    ppermute x3, waiting for transfers between devices: 10.1 us -> 5.04 us  [shards(): going = lax.ppermute(going, 'feat', onward)]
    dot_general x8, matrix products: 9.72 us -> 13.5 us  [term(): jnp.dot(lax.dynamic_index_in_dim(left, owner, 0, keepdims=False), block,...]
    all_to_all x2 -> x1, starting transfers between devices: 11.1 us -> 7.38 us  [shards(): lax.all_to_all(jnp.concatenate([blocks, slot_grads], axis=1), 'feat', spl...]
    all_to_all x1, starting transfers between devices: 5.34 us -> 8.21 us  [shards(): lax.all_to_all(outgoing, 'feat', split_axis=0, concat_axis=0, tiled=True)]
    ppermute x3, waiting for transfers between devices: 0.01 us -> 2.34 us  [shards(): coming = lax.ppermute(coming, 'feat', back)]
    all_to_all x2 -> x1, waiting for transfers between devices: 7.24 us -> 5.29 us  [shards(): lax.all_to_all(jnp.concatenate([blocks, slot_grads], axis=1), 'feat', spl...]
    all_to_all x1, starting transfers between devices: 5.84 us -> 4.03 us  [to_blocks(): lax.all_to_all(columns, 'feat', split_axis=1, concat_axis=0, axis_index_g...]
    dot_general x4 -> x5, matrix products: 9.85 us -> 11.1 us  [contract_lead(): lax.dot_general(left_side, right_side, (((0,), (0,)), ((), ())), preferre...]
  transfers between devices with their start and end apart: 17 -> 16, of which waited for: 8 -> 7; matrix products, arithmetic and copies ran while one was open for 31% -> 34% of each run, Pallas kernels for 20% -> 21%
where the time goes in v4:
time: 164 us; the launch traced here: 163 us
  Pallas kernels  34.1 us (21%)
  starting transfers between devices  33.8 us (21%)
  matrix products  33.2 us (20%)
  waiting for transfers between devices  21.5 us (13%)
  local copies, waits for them, and re-layouts  19.6 us (12%)
  between operations  14.6 us (9%)
  other arithmetic  5.79 us (4%)
    pallas_call x1, Pallas kernels, gather_sum(): pl.pallas_call(add_rows, grid=(targets // step_rows,), out_shape=jax.Shap...  34.1 us
    dot_general x8, matrix products, term(): jnp.dot(lax.dynamic_index_in_dim(left, owner, 0, keepdims=False), block,...  13.5 us
    dot_general x5, matrix products, contract_lead(): lax.dot_general(left_side, right_side, (((0,), (0,)), ((), ())), preferre...  11.1 us
    all_to_all x1, starting transfers between devices, shards(): lax.all_to_all(outgoing, 'feat', split_axis=0, concat_axis=0, tiled=True)  8.21 us
    all_to_all x1, starting transfers between devices, shards(): lax.all_to_all(jnp.concatenate([blocks, slot_grads], axis=1), 'feat', spl...  7.38 us
    all_to_all x1, starting transfers between devices, shards(): lax.all_to_all(side_rows, 'feat', split_axis=0, concat_axis=0, tiled=True)  5.39 us
    all_to_all x1, waiting for transfers between devices, shards(): lax.all_to_all(jnp.concatenate([blocks, slot_grads], axis=1), 'feat', spl...  5.29 us
    ppermute x3, waiting for transfers between devices, shards(): going = lax.ppermute(going, 'feat', onward)  5.04 us
  transfers between devices with their start and end apart: 16, of which 7 were waited for; matrix products, arithmetic and copies ran while one was open for 34% of the time, Pallas kernels for 21%

profile of v4, /device:TPU:1, one launch (start us, length us, event | category | flops | bytes accessed | tf_op | source)
XLA Modules:
  0.0 162.7 jit_solution(2670213924897720062)
XLA Ops:
  10.1 2.4 %convolution_divide_fusion = f32[64,1024]{1,0:T(8,128)S(1)} fusion(bf16[64,1024]{1,0:T(8,128)(2,1)} %param.21, bf16[1024,1024]{1,0:T(8,128)(2,1)} %param.17, f32[64]{0:T(128)S(1)} %convert_element_type.41), kind=kOutput, calls=%fused_computation.11 | convolution fusion | flops 134283264 | bytes 2490624 | tf_op jit(solution)/shard_map/dot_general | solution.py:22
  12.9 1.6 %fusion.53 = (bf16[48,2048]{1,0:T(8,128)(2,1)}, bf16[6,8,16,128]{3,1,2,0:T(8,128)(2,1)S(1)}) fusion(bf16[48,8192]{1,0:T(8,128)(2,1)} %own_ref), kind=kLoop, calls=%fused_computation.91 | loop fusion | bytes 589824 | tf_op jit(solution)/shard_map/slice | solution.py:144
  15.4 7.4 %all-to-all-start = ((bf16[16,64,128]{2,1,0:T(8,128)(2,1)}), bf16[16,64,128]{2,1,0:T(8,128)(2,1)S(1)}, u32[]{:S(2)}, u32[]{:S(2)}) async-start(bf16[16,64,128]{2,1,0:T(8,128)(2,1)} %copy.62), calls=%async_computation | async-start | bytes 524288 | tf_op jit(solution)/shard_map/all_to_all | solution.py:159
  26.5 1.7 %reshape.117 = bf16[48,8,2,128]{3,2,1,0:T(2,128)(2,1)} reshape(bf16[48,2048]{1,0:T(8,128)(2,1)} %get-tuple-element.25) | data formatting | bytes 393216 | tf_op jit(solution)/shard_map/reshape | solution.py:137
  28.2 1.5 fusion.57
  29.7 5.3 %all-to-all-done = bf16[16,64,128]{2,1,0:T(8,128)(2,1)S(1)} async-done(((bf16[16,64,128]{2,1,0:T(8,128)(2,1)}), bf16[16,64,128]{2,1,0:T(8,128)(2,1)S(1)}, u32[]{:S(2)}, u32[]{:S(2)}) %all-to-all-start) | async-done | bytes 262176 | tf_op jit(solution)/shard_map/all_to_all | solution.py:159
  35.7 2.7 %fusion.56 = f32[128,1024]{1,0:T(8,128)} fusion(bf16[768,128]{1,0:T(8,128)(2,1)S(1)} %bitcast.93, bf16[768,1024]{1,0:T(8,128)(2,1)} %param.13), kind=kOutput, calls=%fused_computation.94 | convolution fusion | flops 201326592 | bytes 2293760 | tf_op jit(solution)/shard_map/dot_general | solution.py:16
  38.4 34.1 %gather_sum.1 = f32[1024,128]{1,0:T(8,128)S(1)} custom-call(s32[25,1024]{1,0:T(8,128)S(1)} %bitcast.88, bf16[48,8192]{1,0:T(8,128)(2,1)S(1)} %copy-done.1, bf16[48,8192]{1,0:T(8,128)(2,1)S(1)} %collective-permute-done.partner_ref), custom_call_target="tpu_custom_call" | custom-call | flops 3276800 | bytes 104857600 | tf_op jit(solution)/shard_map/gather_sum/pallas_call | solution.py:72
  75.2 4.0 %all-to-all-start.1 = ((bf16[96,8,128]{2,0,1:T(8,128)(2,1)}), bf16[96,8,128]{2,0,1:T(8,128)(2,1)}, u32[]{:S(2)}, u32[]{:S(2)}) async-start(bf16[96,8,128]{2,0,1:T(8,128)(2,1)} %copy.64), calls=%async_computation.1 | async-start | bytes 393216 | tf_op jit(solution)/shard_map/all_to_all | solution.py:127
  79.3 1.5 constant_dynamic-slice_fusion.8
  83.4 1.6 constant_dynamic-slice_fusion.5
  85.0 3.3 %all-to-all-done.1 = bf16[96,8,128]{2,0,1:T(8,128)(2,1)} async-done(((bf16[96,8,128]{2,0,1:T(8,128)(2,1)}), bf16[96,8,128]{2,0,1:T(8,128)(2,1)}, u32[]{:S(2)}, u32[]{:S(2)}) %all-to-all-start.1) | async-done | bytes 196640 | tf_op jit(solution)/shard_map/all_to_all | solution.py:127
  88.3 2.1 %multiply_convert_fusion = (bf16[128,1024]{1,0:T(8,128)(2,1)S(1)}, f32[128,1024]{1,0:T(8,128)S(1)}) fusion(f32[1024]{0:T(1024)S(1)} %copy-done.16, f32[128,1024]{1,0:T(8,128)S(1)} %copy-done.5, bf16[768,128]{1,0:T(8,128)(2,1)} %bitcast.6, bf16[768,1024]{1,0:T(8,128)(2,1)} %param.14), kind=kOutput, calls=%fused_computation.29 | convolution fusion | flops 202768384 | bytes 3084288 | tf_op jit(solution)/shard_map/dot_general | solution.py:16
  91.4 1.3 fusion.14
  92.6 1.5 collective-permute-start.1
  96.8 2.0 %collective-permute-done.2 = bf16[128,1024]{1,0:T(8,128)(2,1)S(1)} collective-permute-done((bf16[128,1024]{1,0:T(8,128)(2,1)}, bf16[128,1024]{1,0:T(8,128)(2,1)S(1)}, u32[]{:S(2)}, u32[]{:S(2)}) %collective-permute-start.2) | collective-permute-done | bytes 262176 | tf_op jit(solution)/shard_map/ppermute | solution.py:222
  98.8 8.2 %all-to-all-start.2 = ((bf16[16,2,1024]{2,1,0:T(2,128)(2,1)}), bf16[16,2,1024]{2,1,0:T(2,128)(2,1)S(1)}, u32[]{:S(2)}, u32[]{:S(2)}) async-start(bf16[16,2,1024]{2,1,0:T(2,128)(2,1)} %reshape.113), calls=%async_computation.2 | async-start | bytes 131072 | tf_op jit(solution)/shard_map/all_to_all | solution.py:236
  107.0 1.4 collective-permute-start.3
  108.5 2.1 %convolution_add_fusion.1 = f32[192,1024]{1,0:T(8,128)} fusion(f32[192,1024]{1,0:T(8,128)S(1)} %fusion.41, bf16[128,1024]{1,0:T(8,128)(2,1)} %collective-permute-done.1, bf16[192,1,128]{2,1,0:T(2,128)(2,1)} %get-tuple-element.35), kind=kOutput, calls=%fused_computation.6 | convolution fusion | flops 50528256 | bytes 1884160 | tf_op jit(solution)/shard_map/dot_general | solution.py:210
  110.6 2.6 %all-to-all-done.2 = bf16[16,2,1024]{2,1,0:T(2,128)(2,1)S(1)} async-done(((bf16[16,2,1024]{2,1,0:T(2,128)(2,1)}), bf16[16,2,1024]{2,1,0:T(2,128)(2,1)S(1)}, u32[]{:S(2)}, u32[]{:S(2)}) %all-to-all-start.2) | async-done | bytes 65568 | tf_op jit(solution)/shard_map/all_to_all | solution.py:236
  113.3 2.9 %fusion.6 = bf16[64,1024]{1,0:T(8,128)(2,1)} fusion(f32[64,1024]{1,0:T(8,128)S(1)} %fusion.51, bf16[1024,1024]{1,0:T(8,128)(2,1)} %param.17, bf16[32,1024]{1,0:T(8,128)(2,1)S(1)} %reshape.115, f32[64]{0:T(128)} %copy-done.17, f32[64,32]{0,1:T(8,128)S(1)} %convert_reduce_fusion), kind=kOutput, calls=%fused_computation.13 | convolution fusion | flops 138676224 | bytes 2564352 | tf_op jit(solution)/shard_map/dot_general | solution.py:243
  116.6 5.4 %all-to-all-start.3 = ((bf16[16,96,64]{1,2,0:T(8,128)(2,1)}), bf16[16,96,64]{1,2,0:T(8,128)(2,1)S(1)}, u32[]{:S(2)}, u32[]{:S(2)}) async-start(bf16[16,96,64]{1,2,0:T(8,128)(2,1)} %bitcast.12), calls=%async_computation.3 | async-start | bytes 524288 | tf_op jit(solution)/shard_map/all_to_all | solution.py:248
  122.0 1.4 collective-permute-start.5
  123.4 2.1 %fusion.31 = f32[192,1024]{1,0:T(8,128)} fusion(bf16[128,1024]{1,0:T(8,128)(2,1)} %collective-permute-done.4, bf16[192,1,128]{2,1,0:T(2,128)(2,1)S(1)} %copy-done.14), kind=kOutput, calls=%fused_computation.56 | convolution fusion | flops 50331648 | bytes 1097728 | tf_op jit(solution)/shard_map/dot_general | solution.py:210
  125.6 2.1 %fusion.34 = f32[192,1024]{1,0:T(8,128)} fusion(bf16[128,1024]{1,0:T(8,128)(2,1)} %collective-permute-done.3, bf16[192,1,128]{2,1,0:T(2,128)(2,1)S(1)} %copy-done.13), kind=kOutput, calls=%fused_computation.59 | convolution fusion | flops 50331648 | bytes 1097728 | tf_op jit(solution)/shard_map/dot_general | solution.py:210
  127.7 5.0 %collective-permute-done.5 = bf16[128,1024]{1,0:T(8,128)(2,1)S(1)} collective-permute-done((bf16[128,1024]{1,0:T(8,128)(2,1)}, bf16[128,1024]{1,0:T(8,128)(2,1)S(1)}, u32[]{:S(2)}, u32[]{:S(2)}) %collective-permute-start.5) | collective-permute-done | bytes 262176 | tf_op jit(solution)/shard_map/ppermute | solution.py:221
  133.4 2.3 %collective-permute-start.7 = (bf16[64,1024]{1,0:T(8,128)(2,1)}, bf16[64,1024]{1,0:T(8,128)(2,1)}, u32[]{:S(2)}, u32[]{:S(2)}) collective-permute-start(bf16[64,1024]{1,0:T(8,128)(2,1)} %slice.67), channel_id=1, source_target_pairs={{0,4},{1,5},{4,8},{5,9},{8,12},{9,13},{12,14},{13,15},{14,10},{15,... | collective-permute-start | bytes 393224 | tf_op jit(solution)/shard_map/ppermute | solution.py:230
  139.4 2.2 %collective-permute-done.8 = bf16[64,1024]{1,0:T(8,128)(2,1)} collective-permute-done((bf16[64,1024]{1,0:T(8,128)(2,1)}, bf16[64,1024]{1,0:T(8,128)(2,1)}, u32[]{:S(2)}, u32[]{:S(2)}) %collective-permute-start.8) | collective-permute-done | bytes 131104 | tf_op jit(solution)/shard_map/ppermute | solution.py:231
  142.9 2.3 %fusion.4 = f32[192,1024]{1,0:T(8,128)S(1)} fusion(f32[192,1024]{1,0:T(8,128)S(1)} %fusion.17, f32[192,1024]{1,0:T(8,128)} %fusion.25, f32[192,1024]{1,0:T(8,128)} %fusion.28, f32[192,1024]{1,0:T(8,128)} %fusion.31, f32[192,1024]{1,0:T(8,128)} %fusion.34, f32[192,1024]{1,0:T(8,128)S(1)} %copy-done.2, bf16[128,1024]{1,0:T(8,128)(2,1)} %copy-done.9, ...), kind=kOutput, calls=%fused_computation.5 | convolution fusion | flops 51511296 | bytes 5816320 | tf_op jit(solution)/shard_map/dot_general | solution.py:210
  146.9 1.6 %collective-permute-start.9 = (f32[96,1024]{1,0:T(8,128)}, f32[96,1024]{1,0:T(8,128)}, u32[]{:S(2)}, u32[]{:S(2)}) collective-permute-start(f32[96,1024]{1,0:T(8,128)} %slice.70), channel_id=1, source_target_pairs={{0,1},{1,0},{2,3},{3,2},{4,5},{5,4},{6,7},{7,6},{8,9},{9,8},{10,11... | collective-permute-start | bytes 1179656 | tf_op jit(solution)/shard_map/ppermute | solution.py:233
  148.5 2.3 %fusion.59 = f32[64,1024]{1,0:T(8,128)} fusion(bf16[512,64]{1,0:T(8,128)(2,1)S(1)} %bitcast.97, bf16[512,1024]{1,0:T(8,128)(2,1)} %all-gather.5.cloned.1.call-done), kind=kOutput, calls=%fused_computation.97 | convolution fusion | flops 67108864 | bytes 1376256 | tf_op jit(solution)/shard_map/dot_general | solution.py:16
  151.2 2.8 %fusion.58 = f32[64,1024]{1,0:T(8,128)} fusion(bf16[1024,64]{0,1:T(8,128)(2,1)S(1)} %reshape.119, bf16[1024,1024]{1,0:T(8,128)(2,1)} %all-gather.3.cloned.1.call-done), kind=kOutput, calls=%fused_computation.96 | convolution fusion | flops 134217728 | bytes 2490368 | tf_op jit(solution)/shard_map/dot_general | solution.py:16
  (113 shorter events, 27.2 us)
Async XLA Ops:
  7.2 21.1 %copy-start = (bf16[1024,1024]{1,0:T(8,128)(2,1)S(1)}, bf16[1024,1024]{1,0:T(8,128)(2,1)}, u32[]{:S(2)}) copy-start(bf16[1024,1024]{1,0:T(8,128)(2,1)} %param.16) | copy-start | bytes 6291460
  7.2 66.2 %all-gather.3.cloned.1.call-start = ((), (), s32[]{:S(2)}) async-start(), calls=%async_computation.4 | async-start | bytes 2228224 | tf_op jit(solution)/shard_map/all_gather | solution.py:140
  7.9 30.5 %collective-permute-start = (bf16[48,8192]{1,0:T(8,128)(2,1)}, bf16[48,8192]{1,0:T(8,128)(2,1)S(1)}, u32[]{:S(2)}, u32[]{:S(2)}) collective-permute-start(bf16[48,8192]{1,0:T(8,128)(2,1)} %own_ref), channel_id=1, source_target_pairs={{0,1},{1,0},{2,3},{3,2},{4,5},{5,4},{6,7},{7,6},{8,9},{9,8},{10,11... | collective-permute-start | bytes 2359304 | tf_op jit(solution)/shard_map/ppermute | solution.py:143
  8.7 14.1 %copy-start.17 = (f32[64]{0:T(128)}, f32[64]{0:T(128)S(1)}, u32[]{:S(2)}) copy-start(f32[64]{0:T(128)S(1)} %convert_element_type.41) | copy-start | bytes 772
  12.5 10.3 %copy-start.6 = (bf16[64,1024]{1,0:T(8,128)(2,1)S(1)}, bf16[64,1024]{1,0:T(8,128)(2,1)}, u32[]{:S(2)}) copy-start(bf16[64,1024]{1,0:T(8,128)(2,1)} %param.21) | copy-start | bytes 393220
  12.6 11.3 %copy-start.19 = (bf16[1024]{0:T(1024)(128)(2,1)S(1)}, bf16[1024]{0:T(1024)(128)(2,1)}, u32[]{:S(2)}) copy-start(bf16[1024]{0:T(1024)(128)(2,1)} %param.15) | copy-start | bytes 6148
  12.6 11.9 %copy-start.20 = (s32[1,16,2]{1,2,0:T(2,128)S(1)}, s32[1,16,2]{1,2,0:T(2,128)}, u32[]{:S(2)}) copy-start(s32[1,16,2]{1,2,0:T(2,128)} %param.18) | copy-start | bytes 388
  15.4 19.6 %all-to-all-start = ((bf16[16,64,128]{2,1,0:T(8,128)(2,1)}), bf16[16,64,128]{2,1,0:T(8,128)(2,1)S(1)}, u32[]{:S(2)}, u32[]{:S(2)}) async-start(bf16[16,64,128]{2,1,0:T(8,128)(2,1)} %copy.62), calls=%async_computation | async-start | bytes 524288 | tf_op jit(solution)/shard_map/all_to_all | solution.py:159
  22.8 125.7 %all-gather.5.cloned.1.call-start = ((), (), s32[]{:S(2)}) async-start(), calls=%async_computation.5 | async-start | bytes 1114112 | tf_op jit(solution)/shard_map/all_gather | solution.py:190
  74.4 7.1 %copy-start.8 = (bf16[48,1024]{0,1:T(8,128)(2,1)S(1)}, bf16[48,1024]{0,1:T(8,128)(2,1)}, u32[]{:S(2)}) copy-start(bf16[48,1024]{0,1:T(8,128)(2,1)} %get-tuple-element.37) | copy-start | bytes 294916
  74.4 7.8 %copy-start.7 = (bf16[48,1024]{0,1:T(8,128)(2,1)S(1)}, bf16[48,1024]{0,1:T(8,128)(2,1)}, u32[]{:S(2)}) copy-start(bf16[48,1024]{0,1:T(8,128)(2,1)} %get-tuple-element.40) | copy-start | bytes 294916
  75.2 13.0 %all-to-all-start.1 = ((bf16[96,8,128]{2,0,1:T(8,128)(2,1)}), bf16[96,8,128]{2,0,1:T(8,128)(2,1)}, u32[]{:S(2)}, u32[]{:S(2)}) async-start(bf16[96,8,128]{2,0,1:T(8,128)(2,1)} %copy.64), calls=%async_computation.1 | async-start | bytes 393216 | tf_op jit(solution)/shard_map/all_to_all | solution.py:127
  79.3 9.0 %copy-start.5 = (f32[128,1024]{1,0:T(8,128)S(1)}, f32[128,1024]{1,0:T(8,128)}, u32[]{:S(2)}) copy-start(f32[128,1024]{1,0:T(8,128)} %fusion.56) | copy-start | bytes 1572868
  79.3 9.0 %copy-start.16 = (f32[1024]{0:T(1024)S(1)}, f32[1024]{0:T(1024)}, u32[]{:S(2)}) copy-start(f32[1024]{0:T(1024)} %convert_element_type.44) | copy-start | bytes 12292
  92.6 6.1 %collective-permute-start.2 = (bf16[128,1024]{1,0:T(8,128)(2,1)}, bf16[128,1024]{1,0:T(8,128)(2,1)S(1)}, u32[]{:S(2)}, u32[]{:S(2)}) collective-permute-start(bf16[128,1024]{1,0:T(8,128)(2,1)} %fusion.14), channel_id=1, source_target_pairs={{4,0},{5,1},{8,4},{9,5},{12,8},{13,9},{14,12},{15,13},{10,14},{11,... | collective-permute-start | bytes 786440 | tf_op jit(solution)/shard_map/ppermute | solution.py:222
  92.6 6.1 %collective-permute-start.1 = (bf16[128,1024]{1,0:T(8,128)(2,1)}, bf16[128,1024]{1,0:T(8,128)(2,1)}, u32[]{:S(2)}, u32[]{:S(2)}) collective-permute-start(bf16[128,1024]{1,0:T(8,128)(2,1)} %fusion.14), channel_id=1, source_target_pairs={{0,4},{1,5},{4,8},{5,9},{8,12},{9,13},{12,14},{13,15},{14,10},{15,... | collective-permute-start | bytes 786440 | tf_op jit(solution)/shard_map/ppermute | solution.py:221
  98.8 17.4 %copy-start.9 = (bf16[128,1024]{1,0:T(8,128)(2,1)}, bf16[128,1024]{1,0:T(8,128)(2,1)S(1)}, u32[]{:S(2)}) copy-start(bf16[128,1024]{1,0:T(8,128)(2,1)S(1)} %collective-permute-done.2) | copy-start | bytes 786436
  98.8 14.5 %all-to-all-start.2 = ((bf16[16,2,1024]{2,1,0:T(2,128)(2,1)}), bf16[16,2,1024]{2,1,0:T(2,128)(2,1)S(1)}, u32[]{:S(2)}, u32[]{:S(2)}) async-start(bf16[16,2,1024]{2,1,0:T(2,128)(2,1)} %reshape.113), calls=%async_computation.2 | async-start | bytes 131072 | tf_op jit(solution)/shard_map/all_to_all | solution.py:236
  107.0 9.2 %collective-permute-start.3 = (bf16[128,1024]{1,0:T(8,128)(2,1)}, bf16[128,1024]{1,0:T(8,128)(2,1)}, u32[]{:S(2)}, u32[]{:S(2)}) collective-permute-start(bf16[128,1024]{1,0:T(8,128)(2,1)} %collective-permute-done.1), channel_id=1, source_target_pairs={{0,4},{1,5},{4,8},{5,9},{8,12},{9,13},{12,14},{13,15},{14,10},{15,... | collective-permute-start | bytes 786440 | tf_op jit(solution)/shard_map/ppermute | solution.py:221
  108.4 8.2 %collective-permute-start.4 = (bf16[128,1024]{1,0:T(8,128)(2,1)S(1)}, bf16[128,1024]{1,0:T(8,128)(2,1)}, u32[]{:S(2)}, u32[]{:S(2)}) collective-permute-start(bf16[128,1024]{1,0:T(8,128)(2,1)S(1)} %collective-permute-done.2), channel_id=1, source_target_pairs={{4,0},{5,1},{8,4},{9,5},{12,8},{13,9},{14,12},{15,13},{10,14},{11,... | collective-permute-start | bytes 786440 | tf_op jit(solution)/shard_map/ppermute | solution.py:222
  110.6 12.9 %copy-start.14 = (bf16[192,1,128]{2,1,0:T(2,128)(2,1)S(1)}, bf16[192,1,128]{2,1,0:T(2,128)(2,1)}, u32[]{:S(2)}) copy-start(bf16[192,1,128]{2,1,0:T(2,128)(2,1)} %get-tuple-element.33) | copy-start | bytes 147460
  113.3 12.3 %copy-start.13 = (bf16[192,1,128]{2,1,0:T(2,128)(2,1)S(1)}, bf16[192,1,128]{2,1,0:T(2,128)(2,1)}, u32[]{:S(2)}) copy-start(bf16[192,1,128]{2,1,0:T(2,128)(2,1)} %get-tuple-element.34) | copy-start | bytes 147460
  116.2 20.5 %copy-start.12 = (bf16[192,1,128]{2,1,0:T(2,128)(2,1)S(1)}, bf16[192,1,128]{2,1,0:T(2,128)(2,1)}, u32[]{:S(2)}) copy-start(bf16[192,1,128]{2,1,0:T(2,128)(2,1)} %get-tuple-element.31) | copy-start | bytes 147460
  116.6 21.2 %copy-start.11 = (bf16[192,1,128]{2,1,0:T(2,128)(2,1)S(1)}, bf16[192,1,128]{2,1,0:T(2,128)(2,1)}, u32[]{:S(2)}) copy-start(bf16[192,1,128]{2,1,0:T(2,128)(2,1)} %get-tuple-element.32) | copy-start | bytes 147460
  116.6 22.4 %all-to-all-start.3 = ((bf16[16,96,64]{1,2,0:T(8,128)(2,1)}), bf16[16,96,64]{1,2,0:T(8,128)(2,1)S(1)}, u32[]{:S(2)}, u32[]{:S(2)}) async-start(bf16[16,96,64]{1,2,0:T(8,128)(2,1)} %bitcast.12), calls=%async_computation.3 | async-start | bytes 524288 | tf_op jit(solution)/shard_map/all_to_all | solution.py:248
  122.0 10.8 %collective-permute-start.5 = (bf16[128,1024]{1,0:T(8,128)(2,1)}, bf16[128,1024]{1,0:T(8,128)(2,1)S(1)}, u32[]{:S(2)}, u32[]{:S(2)}) collective-permute-start(bf16[128,1024]{1,0:T(8,128)(2,1)} %collective-permute-done.3), channel_id=1, source_target_pairs={{0,4},{1,5},{4,8},{5,9},{8,12},{9,13},{12,14},{13,15},{14,10},{15,... | collective-permute-start | bytes 786440 | tf_op jit(solution)/shard_map/ppermute | solution.py:221
  123.4 12.4 %collective-permute-start.6 = (bf16[128,1024]{1,0:T(8,128)(2,1)}, bf16[128,1024]{1,0:T(8,128)(2,1)S(1)}, u32[]{:S(2)}, u32[]{:S(2)}) collective-permute-start(bf16[128,1024]{1,0:T(8,128)(2,1)} %collective-permute-done.4), channel_id=1, source_target_pairs={{4,0},{5,1},{8,4},{9,5},{12,8},{13,9},{14,12},{15,13},{10,14},{11,... | collective-permute-start | bytes 786440 | tf_op jit(solution)/shard_map/ppermute | solution.py:222
  133.4 6.0 %collective-permute-start.7 = (bf16[64,1024]{1,0:T(8,128)(2,1)}, bf16[64,1024]{1,0:T(8,128)(2,1)}, u32[]{:S(2)}, u32[]{:S(2)}) collective-permute-start(bf16[64,1024]{1,0:T(8,128)(2,1)} %slice.67), channel_id=1, source_target_pairs={{0,4},{1,5},{4,8},{5,9},{8,12},{9,13},{12,14},{13,15},{14,10},{15,... | collective-permute-start | bytes 393224 | tf_op jit(solution)/shard_map/ppermute | solution.py:230
  136.4 5.2 %collective-permute-start.8 = (bf16[64,1024]{1,0:T(8,128)(2,1)}, bf16[64,1024]{1,0:T(8,128)(2,1)}, u32[]{:S(2)}, u32[]{:S(2)}) collective-permute-start(bf16[64,1024]{1,0:T(8,128)(2,1)} %slice.68), channel_id=1, source_target_pairs={{4,0},{5,1},{8,4},{9,5},{12,8},{13,9},{14,12},{15,13},{10,14},{11,... | collective-permute-start | bytes 393224 | tf_op jit(solution)/shard_map/ppermute | solution.py:231
  136.7 6.2 %copy-start.2 = (f32[192,1024]{1,0:T(8,128)S(1)}, f32[192,1024]{1,0:T(8,128)}, u32[]{:S(2)}) copy-start(f32[192,1024]{1,0:T(8,128)} %convolution_add_fusion.1) | copy-start | bytes 2359300
  146.9 7.1 %collective-permute-start.9 = (f32[96,1024]{1,0:T(8,128)}, f32[96,1024]{1,0:T(8,128)}, u32[]{:S(2)}, u32[]{:S(2)}) collective-permute-start(f32[96,1024]{1,0:T(8,128)} %slice.70), channel_id=1, source_target_pairs={{0,1},{1,0},{2,3},{3,2},{4,5},{5,4},{6,7},{7,6},{8,9},{9,8},{10,11... | collective-permute-start | bytes 1179656 | tf_op jit(solution)/shard_map/ppermute | solution.py:233
  148.5 5.5 %copy-start.4 = (f32[192,1024]{1,0:T(8,128)S(1)}, f32[192,1024]{1,0:T(8,128)}, u32[]{:S(2)}) copy-start(f32[192,1024]{1,0:T(8,128)} %copy-done.3) | copy-start | bytes 2359300
  (5 other events, 6.1 us)
Sparse Core Ops, SparseCore 0:
  10.2 45.5 all-gather.2
  57.9 38.3 all-gather.4

commit v5 on v4

--- a/solution.py
+++ b/solution.py
@@ -215,14 +215,14 @@
 
     side_rows = jnp.concatenate([seed_hidden, sent_rows], axis=0)
     side_rows = jnp.transpose(side_rows.reshape(own_seeds + slot_total, devices, -1), (1, 0, 2))
+    outgoing = outgoing.reshape(devices, -1, side_rows.shape[2])
+    side_rows = jnp.concatenate([side_rows, outgoing], axis=1)
     total = term(0, grad_pre)
     going, coming = grad_pre, grad_pre
     for hop in range(1, (pairs + 1) // 2):
         going = lax.ppermute(going, "feat", onward)
         coming = lax.ppermute(coming, "feat", back)
         if hop == 1:
-            outgoing, going, coming = lax.optimization_barrier((outgoing, going, coming))
-        if hop == 2:
             side_rows, going, coming = lax.optimization_barrier((side_rows, going, coming))
         total = total + term(-hop, going) + term(hop, coming)
     if pairs % 2 == 0:
@@ -233,7 +233,8 @@
     from_other = lax.ppermute(total[: 2 * width], "feat", swap)
     both_one = total[2 * width :] + from_other
 
-    incoming = lax.all_to_all(outgoing, "feat", split_axis=0, concat_axis=0, tiled=True)
+    side_rows = lax.all_to_all(side_rows, "feat", split_axis=0, concat_axis=0, tiled=True)
+    incoming = side_rows[:, own_seeds + slot_total :]
     summed_two = jnp.dot(
         ref_count.astype(jnp.bfloat16),
         incoming.reshape(slot_total, hidden_width),
@@ -245,10 +246,9 @@
     )
     layer_out = out_full.astype(jnp.bfloat16)
 
-    side_rows = lax.all_to_all(side_rows, "feat", split_axis=0, concat_axis=0, tiled=True)
     slice_two = side_rows.shape[2]
     seed_cols = side_rows[:, :own_seeds].reshape(-1, slice_two)
-    sent_cols = side_rows[:, own_seeds:].reshape(devices, devices, slots_peer, slice_two)
+    sent_cols = side_rows[:, own_seeds : own_seeds + slot_total].reshape(devices, devices, slots_peer, slice_two)
     sent_cols = jnp.transpose(sent_cols, (1, 0, 2, 3)).reshape(-1, slice_two)
     return (
         layer_out,

time: 164 us -> 150 us (0.915)
  waiting for transfers between devices: 21.5 us -> 13.7 us
  starting transfers between devices: 33.8 us -> 26.8 us
    all_to_all x1 -> x0, starting transfers between devices: 8.21 us -> none  [shards(): lax.all_to_all(outgoing, 'feat', split_axis=0, concat_axis=0, tiled=True)]
    ppermute x3, waiting for transfers between devices: 5.04 us -> 0.32 us  [shards(): going = lax.ppermute(going, 'feat', onward)]
    all_to_all x1 -> x0, waiting for transfers between devices: 2.64 us -> none  [shards(): lax.all_to_all(outgoing, 'feat', split_axis=0, concat_axis=0, tiled=True)]
    dot_general x8, matrix products: 13.5 us -> 10.9 us  [term(): jnp.dot(lax.dynamic_index_in_dim(left, owner, 0, keepdims=False), block,...]
    all_to_all x1, starting transfers between devices: 5.39 us -> 7.33 us  [shards(): lax.all_to_all(side_rows, 'feat', split_axis=0, concat_axis=0, tiled=True)]
  transfers between devices with their start and end apart: 16 -> 15, of which waited for: 7 -> 7; matrix products, arithmetic and copies ran while one was open for 34% -> 38% of each run, Pallas kernels for 21% -> 23%
where the time goes in v5:
time: 150 us; the launch traced here: 149 us
  Pallas kernels  34.1 us (23%)
  matrix products  31.6 us (21%)
  starting transfers between devices  26.8 us (18%)
  local copies, waits for them, and re-layouts  20.6 us (14%)
  between operations  14.7 us (10%)
  waiting for transfers between devices  13.7 us (9%)
  other arithmetic  7.34 us (5%)
    pallas_call x1, Pallas kernels, gather_sum(): pl.pallas_call(add_rows, grid=(targets // step_rows,), out_shape=jax.Shap...  34.1 us
    dot_general x5, matrix products, contract_lead(): lax.dot_general(left_side, right_side, (((0,), (0,)), ((), ())), preferre...  12.2 us
    dot_general x8, matrix products, term(): jnp.dot(lax.dynamic_index_in_dim(left, owner, 0, keepdims=False), block,...  10.9 us
    all_to_all x1, starting transfers between devices, shards(): lax.all_to_all(jnp.concatenate([blocks, slot_grads], axis=1), 'feat', spl...  7.38 us
    all_to_all x1, starting transfers between devices, shards(): lax.all_to_all(side_rows, 'feat', split_axis=0, concat_axis=0, tiled=True)  7.33 us
    ppermute x3, starting transfers between devices, shards(): going = lax.ppermute(going, 'feat', onward)  4.11 us
    all_to_all x1, starting transfers between devices, to_blocks(): lax.all_to_all(columns, 'feat', split_axis=1, concat_axis=0, axis_index_g...  4.03 us
    all_to_all x1, waiting for transfers between devices, shards(): lax.all_to_all(jnp.concatenate([blocks, slot_grads], axis=1), 'feat', spl...  3.93 us
  transfers between devices with their start and end apart: 15, of which 7 were waited for; matrix products, arithmetic and copies ran while one was open for 38% of the time, Pallas kernels for 23%

profile of v5, /device:TPU:1, one launch (start us, length us, event | category | flops | bytes accessed | tf_op | source)
XLA Modules:
  0.0 148.8 jit_solution(5208797793920976614)
XLA Ops:
  10.1 2.4 %convolution_divide_fusion = f32[64,1024]{1,0:T(8,128)S(1)} fusion(bf16[64,1024]{1,0:T(8,128)(2,1)} %param.21, bf16[1024,1024]{1,0:T(8,128)(2,1)} %param.17, f32[64]{0:T(128)S(1)} %convert_element_type.41), kind=kOutput, calls=%fused_computation.11 | convolution fusion | flops 134283264 | bytes 2490624 | tf_op jit(solution)/shard_map/dot_general | solution.py:22
  12.9 1.6 %fusion.51 = (bf16[48,2048]{1,0:T(8,128)(2,1)}, bf16[6,8,16,128]{3,1,2,0:T(8,128)(2,1)S(1)}) fusion(bf16[48,8192]{1,0:T(8,128)(2,1)} %own_ref), kind=kLoop, calls=%fused_computation.91 | loop fusion | bytes 589824 | tf_op jit(solution)/shard_map/slice | solution.py:144
  15.4 7.4 %all-to-all-start = ((bf16[16,64,128]{2,1,0:T(8,128)(2,1)}), bf16[16,64,128]{2,1,0:T(8,128)(2,1)S(1)}, u32[]{:S(2)}, u32[]{:S(2)}) async-start(bf16[16,64,128]{2,1,0:T(8,128)(2,1)} %copy.69), calls=%async_computation | async-start | bytes 524288 | tf_op jit(solution)/shard_map/all_to_all | solution.py:159
  23.9 1.1 reshape.108
  25.2 1.7 %reshape.114 = bf16[48,8,2,128]{3,2,1,0:T(2,128)(2,1)} reshape(bf16[48,2048]{1,0:T(8,128)(2,1)} %get-tuple-element.19) | data formatting | bytes 393216 | tf_op jit(solution)/shard_map/reshape | solution.py:137
  26.9 1.3 convert_element_type.44
  29.6 1.5 fusion.56
  31.0 3.9 %all-to-all-done = bf16[16,64,128]{2,1,0:T(8,128)(2,1)S(1)} async-done(((bf16[16,64,128]{2,1,0:T(8,128)(2,1)}), bf16[16,64,128]{2,1,0:T(8,128)(2,1)S(1)}, u32[]{:S(2)}, u32[]{:S(2)}) %all-to-all-start) | async-done | bytes 262176 | tf_op jit(solution)/shard_map/all_to_all | solution.py:159
  35.6 2.7 %fusion.55 = f32[128,1024]{1,0:T(8,128)} fusion(bf16[768,128]{1,0:T(8,128)(2,1)S(1)} %bitcast.94, bf16[768,1024]{1,0:T(8,128)(2,1)} %param.13), kind=kOutput, calls=%fused_computation.95 | convolution fusion | flops 201326592 | bytes 2293760 | tf_op jit(solution)/shard_map/dot_general | solution.py:16
  38.3 34.1 %gather_sum.1 = f32[1024,128]{1,0:T(8,128)S(1)} custom-call(s32[25,1024]{1,0:T(8,128)S(1)} %bitcast.88, bf16[48,8192]{1,0:T(8,128)(2,1)S(1)} %copy-done.1, bf16[48,8192]{1,0:T(8,128)(2,1)S(1)} %collective-permute-done.partner_ref), custom_call_target="tpu_custom_call" | custom-call | flops 3276800 | bytes 104857600 | tf_op jit(solution)/shard_map/gather_sum/pallas_call | solution.py:72
  75.2 4.0 %all-to-all-start.1 = ((bf16[96,8,128]{2,0,1:T(8,128)(2,1)}), bf16[96,8,128]{2,0,1:T(8,128)(2,1)}, u32[]{:S(2)}, u32[]{:S(2)}) async-start(bf16[96,8,128]{2,0,1:T(8,128)(2,1)} %copy.71), calls=%async_computation.1 | async-start | bytes 393216 | tf_op jit(solution)/shard_map/all_to_all | solution.py:127
  79.3 1.5 %constant_dynamic-slice_fusion.8 = (bf16[48,8,1,128]{3,2,1,0:T(2,128)(2,1)S(1)}, bf16[48,8,1,128]{3,2,1,0:T(2,128)(2,1)S(1)}) fusion(bf16[48,8,2,128]{3,2,1,0:T(2,128)(2,1)} %reshape.114, s32[]{:T(128)S(6)} %select_n.92, bf16[48,8,2,128]{3,2,1,0:T(2,128)(2,1)} %reshape.113), kind=kLoop, calls=%fused_computation.84 | loop fusion | bytes 393220 | tf_op jit(solution)/shard_map/jit(dynamic_index_in_dim)/dynamic_slice | solution.py:138
  83.4 1.6 %constant_dynamic-slice_fusion.2 = (bf16[192,1,128]{2,1,0:T(2,128)(2,1)}, bf16[192,1,128]{2,1,0:T(2,128)(2,1)}, bf16[192,1,128]{2,1,0:T(2,128)(2,1)}, bf16[192,1...) fusion(bf16[192,8,128]{2,1,0:T(8,128)(2,1)S(1)} %pad_maximum_fu, ...), kind=kLoop, calls=%fused_computation.78 | loop fusion | bytes 786464 | tf_op jit(solution)/shard_map/dynamic-slice.5
  85.0 3.0 %all-to-all-done.1 = bf16[96,8,128]{2,0,1:T(8,128)(2,1)} async-done(((bf16[96,8,128]{2,0,1:T(8,128)(2,1)}), bf16[96,8,128]{2,0,1:T(8,128)(2,1)}, u32[]{:S(2)}, u32[]{:S(2)}) %all-to-all-start.1) | async-done | bytes 196640 | tf_op jit(solution)/shard_map/all_to_all | solution.py:127
  88.0 2.1 %multiply_convert_fusion = (bf16[128,1024]{1,0:T(8,128)(2,1)S(1)}, f32[128,1024]{1,0:T(8,128)S(1)}) fusion(f32[1024]{0:T(1024)S(1)} %copy-done.15, f32[128,1024]{1,0:T(8,128)S(1)} %copy-done.5, bf16[768,128]{1,0:T(8,128)(2,1)} %bitcast.6, bf16[768,1024]{1,0:T(8,128)(2,1)} %param.14), kind=kOutput, calls=%fused_computation.29 | convolution fusion | flops 202768384 | bytes 3084288 | tf_op jit(solution)/shard_map/dot_general | solution.py:16
  90.1 2.3 %fusion.13 = bf16[128,1024]{1,0:T(8,128)(2,1)} fusion(f32[128,1024]{1,0:T(8,128)S(1)} %get-tuple-element.38, bf16[32,1024]{1,0:T(8,128)(2,1)} %reshape.111, f32[64,1024]{1,0:T(8,128)} %fusion.56, s32[32]{0:T(128)S(1)} %copy-done.17), kind=kOutput, calls=%fused_computation.26 | convolution fusion | flops 11145216 | bytes 1114240 | tf_op jit(solution)/shard_map/dot_general | solution.py:16
  95.9 2.1 %fusion.39 = f32[192,1024]{1,0:T(8,128)} fusion(bf16[128,1024]{1,0:T(8,128)(2,1)} %fusion.13, bf16[192,1,128]{2,1,0:T(2,128)(2,1)S(1)} %copy-done.12), kind=kOutput, calls=%fused_computation.66 | convolution fusion | flops 50331648 | bytes 1097728 | tf_op jit(solution)/shard_map/dot_general | solution.py:210
  99.3 2.1 %collective-permute-start.3 = (bf16[128,1024]{1,0:T(8,128)(2,1)}, bf16[128,1024]{1,0:T(8,128)(2,1)}, u32[]{:S(2)}, u32[]{:S(2)}) collective-permute-start(bf16[128,1024]{1,0:T(8,128)(2,1)} %collective-permute-done.1), channel_id=1, source_target_pairs={{0,4},{1,5},{4,8},{5,9},{8,12},{9,13},{12,14},{13,15},{14,10},{15,... | collective-permute-start | bytes 786440 | tf_op jit(solution)/shard_map/ppermute | solution.py:223
  101.4 7.3 %all-to-all-start.2 = ((bf16[16,128,64]{1,2,0:T(8,128)(2,1)}), bf16[16,128,64]{1,2,0:T(8,128)(2,1)S(1)}, u32[]{:S(2)}, u32[]{:S(2)}) async-start(bf16[16,128,64]{1,2,0:T(8,128)(2,1)} %pad_maximum_fusion.3), calls=%async_computation.2 | async-start | bytes 524288 | tf_op jit(solution)/shard_map/all_to_all | solution.py:236
  108.8 1.5 %convolution_add_fusion.2 = f32[192,1024]{1,0:T(8,128)S(1)} fusion(f32[192,1024]{1,0:T(8,128)} %fusion.39, bf16[128,1024]{1,0:T(8,128)(2,1)} %collective-permute-done.1, bf16[192,1,128]{2,1,0:T(2,128)(2,1)} %get-tuple-element.29), kind=kOutput, calls=%fused_computation.6 | convolution fusion | flops 50528256 | bytes 1884160 | tf_op jit(solution)/shard_map/dot_general | solution.py:210
  110.3 1.4 collective-permute-start.5
  111.8 1.2 fusion.32
  113.2 1.2 fusion.29
  114.4 2.1 %fusion.3 = f32[192,1024]{1,0:T(8,128)} fusion(f32[192,1024]{1,0:T(8,128)S(1)} %fusion.29, f32[192,1024]{1,0:T(8,128)S(1)} %fusion.32, f32[192,1024]{1,0:T(8,128)S(1)} %convolution_add_fusion.2, bf16[128,1024]{1,0:T(8,128)(2,1)} %collective-permute-done.2, bf16[192,1,128]{2,1,0:T(2,128)(2,1)S(1)} %copy-done.14), kind=kOutput, calls=%fused_computation.5 | convolution fusion | flops 50921472 | bytes 3457024 | tf_op jit(solution)/shard_map/dot_general | solution.py:210
  116.5 1.5 all-to-all-done.2
  119.5 2.9 %fusion.57 = f32[64,1024]{1,0:T(8,128)} fusion(bf16[1024,64]{0,1:T(8,128)(2,1)S(1)} %reshape.115, bf16[1024,1024]{1,0:T(8,128)(2,1)} %all-gather.3.cloned.1.call-done), kind=kOutput, calls=%fused_computation.97 | convolution fusion | flops 134217728 | bytes 2490368 | tf_op jit(solution)/shard_map/dot_general | solution.py:16
  123.3 1.2 collective-permute-start.7
  125.8 1.2 fusion.24
  127.4 2.8 %collective-permute-done.8 = bf16[64,1024]{1,0:T(8,128)(2,1)S(1)} collective-permute-done((bf16[64,1024]{1,0:T(8,128)(2,1)S(1)}, bf16[64,1024]{1,0:T(8,128)(2,1)S(1)}, u32[]{:S(2)}, u32[]{:S(2)}) %collective-permute-start.8) | collective-permute-done | bytes 131104 | tf_op jit(solution)/shard_map/ppermute | solution.py:231
  130.6 1.2 fusion.1
  134.6 2.3 %fusion.58 = f32[64,1024]{1,0:T(8,128)} fusion(bf16[512,64]{1,0:T(8,128)(2,1)S(1)} %bitcast.98, bf16[512,1024]{1,0:T(8,128)(2,1)} %all-gather.5.cloned.1.call-done), kind=kOutput, calls=%fused_computation.98 | convolution fusion | flops 67108864 | bytes 1376256 | tf_op jit(solution)/shard_map/dot_general | solution.py:16
  137.2 2.9 %fusion.5 = bf16[64,1024]{1,0:T(8,128)(2,1)} fusion(f32[64,1024]{1,0:T(8,128)S(1)} %fusion.49, bf16[1024,1024]{1,0:T(8,128)(2,1)} %param.17, bf16[32,1024]{1,0:T(8,128)(2,1)S(1)} %reshape.112, f32[64]{0:T(128)} %copy-done.16, f32[64,32]{0,1:T(8,128)S(1)} %convert_reduce_fusion), kind=kOutput, calls=%fused_computation.13 | convolution fusion | flops 138676224 | bytes 2564352 | tf_op jit(solution)/shard_map/dot_general | solution.py:244
  (108 shorter events, 26.8 us)
Async XLA Ops:
  7.2 22.4 %copy-start = (bf16[1024,1024]{1,0:T(8,128)(2,1)S(1)}, bf16[1024,1024]{1,0:T(8,128)(2,1)}, u32[]{:S(2)}) copy-start(bf16[1024,1024]{1,0:T(8,128)(2,1)} %param.16) | copy-start | bytes 6291460
  7.2 66.2 %all-gather.3.cloned.1.call-start = ((), (), s32[]{:S(2)}) async-start(), calls=%async_computation.3 | async-start | bytes 2228224 | tf_op jit(solution)/shard_map/all_gather | solution.py:140
  7.9 30.4 %collective-permute-start = (bf16[48,8192]{1,0:T(8,128)(2,1)}, bf16[48,8192]{1,0:T(8,128)(2,1)S(1)}, u32[]{:S(2)}, u32[]{:S(2)}) collective-permute-start(bf16[48,8192]{1,0:T(8,128)(2,1)} %own_ref), channel_id=1, source_target_pairs={{0,1},{1,0},{2,3},{3,2},{4,5},{5,4},{6,7},{7,6},{8,9},{9,8},{10,11... | collective-permute-start | bytes 2359304 | tf_op jit(solution)/shard_map/ppermute | solution.py:143
  8.7 14.1 %copy-start.16 = (f32[64]{0:T(128)}, f32[64]{0:T(128)S(1)}, u32[]{:S(2)}) copy-start(f32[64]{0:T(128)S(1)} %convert_element_type.41) | copy-start | bytes 772
  12.5 10.3 %copy-start.6 = (bf16[64,1024]{1,0:T(8,128)(2,1)S(1)}, bf16[64,1024]{1,0:T(8,128)(2,1)}, u32[]{:S(2)}) copy-start(bf16[64,1024]{1,0:T(8,128)(2,1)} %param.21) | copy-start | bytes 393220
  15.4 19.6 %all-to-all-start = ((bf16[16,64,128]{2,1,0:T(8,128)(2,1)}), bf16[16,64,128]{2,1,0:T(8,128)(2,1)S(1)}, u32[]{:S(2)}, u32[]{:S(2)}) async-start(bf16[16,64,128]{2,1,0:T(8,128)(2,1)} %copy.69), calls=%async_computation | async-start | bytes 524288 | tf_op jit(solution)/shard_map/all_to_all | solution.py:159
  22.8 111.9 %all-gather.5.cloned.1.call-start = ((), (), s32[]{:S(2)}) async-start(), calls=%async_computation.4 | async-start | bytes 1114112 | tf_op jit(solution)/shard_map/all_gather | solution.py:190
  35.6 2.7 %copy-start.1 = (bf16[48,8192]{1,0:T(8,128)(2,1)S(1)}, bf16[48,8192]{1,0:T(8,128)(2,1)}, u32[]{:S(2)}) copy-start(bf16[48,8192]{1,0:T(8,128)(2,1)} %own_ref) | copy-start | bytes 2359300
  74.4 7.1 %copy-start.8 = (bf16[48,1024]{0,1:T(8,128)(2,1)S(1)}, bf16[48,1024]{0,1:T(8,128)(2,1)}, u32[]{:S(2)}) copy-start(bf16[48,1024]{0,1:T(8,128)(2,1)} %get-tuple-element.33) | copy-start | bytes 294916
  74.4 7.8 %copy-start.7 = (bf16[48,1024]{0,1:T(8,128)(2,1)S(1)}, bf16[48,1024]{0,1:T(8,128)(2,1)}, u32[]{:S(2)}) copy-start(bf16[48,1024]{0,1:T(8,128)(2,1)} %get-tuple-element.36) | copy-start | bytes 294916
  75.2 12.8 %all-to-all-start.1 = ((bf16[96,8,128]{2,0,1:T(8,128)(2,1)}), bf16[96,8,128]{2,0,1:T(8,128)(2,1)}, u32[]{:S(2)}, u32[]{:S(2)}) async-start(bf16[96,8,128]{2,0,1:T(8,128)(2,1)} %copy.71), calls=%async_computation.1 | async-start | bytes 393216 | tf_op jit(solution)/shard_map/all_to_all | solution.py:127
  79.3 8.7 %copy-start.5 = (f32[128,1024]{1,0:T(8,128)S(1)}, f32[128,1024]{1,0:T(8,128)}, u32[]{:S(2)}) copy-start(f32[128,1024]{1,0:T(8,128)} %fusion.55) | copy-start | bytes 1572868
  79.3 8.7 %copy-start.15 = (f32[1024]{0:T(1024)S(1)}, f32[1024]{0:T(1024)}, u32[]{:S(2)}) copy-start(f32[1024]{0:T(1024)} %convert_element_type.44) | copy-start | bytes 12292
  83.4 6.7 %copy-start.17 = (s32[32]{0:T(128)S(1)}, s32[32]{0:T(128)}, u32[]{:S(2)}) copy-start(s32[32]{0:T(128)} %eq.42) | copy-start | bytes 388
  92.3 6.0 %collective-permute-start.1 = (bf16[128,1024]{1,0:T(8,128)(2,1)}, bf16[128,1024]{1,0:T(8,128)(2,1)}, u32[]{:S(2)}, u32[]{:S(2)}) collective-permute-start(bf16[128,1024]{1,0:T(8,128)(2,1)} %fusion.13), channel_id=1, source_target_pairs={{0,4},{1,5},{4,8},{5,9},{8,12},{9,13},{12,14},{13,15},{14,10},{15,... | collective-permute-start | bytes 786440 | tf_op jit(solution)/shard_map/ppermute | solution.py:223
  92.9 6.4 %collective-permute-start.2 = (bf16[128,1024]{1,0:T(8,128)(2,1)}, bf16[128,1024]{1,0:T(8,128)(2,1)}, u32[]{:S(2)}, u32[]{:S(2)}) collective-permute-start(bf16[128,1024]{1,0:T(8,128)(2,1)} %fusion.13), channel_id=1, source_target_pairs={{4,0},{5,1},{8,4},{9,5},{12,8},{13,9},{14,12},{15,13},{10,14},{11,... | collective-permute-start | bytes 786440 | tf_op jit(solution)/shard_map/ppermute | solution.py:224
  94.0 1.9 %copy-start.12 = (bf16[192,1,128]{2,1,0:T(2,128)(2,1)S(1)}, bf16[192,1,128]{2,1,0:T(2,128)(2,1)}, u32[]{:S(2)}) copy-start(bf16[192,1,128]{2,1,0:T(2,128)(2,1)} %get-tuple-element.30) | copy-start | bytes 147460
  95.1 16.7 %copy-start.11 = (bf16[192,1,128]{2,1,0:T(2,128)(2,1)S(1)}, bf16[192,1,128]{2,1,0:T(2,128)(2,1)}, u32[]{:S(2)}) copy-start(bf16[192,1,128]{2,1,0:T(2,128)(2,1)} %get-tuple-element.27) | copy-start | bytes 147460
  99.3 11.0 %collective-permute-start.3 = (bf16[128,1024]{1,0:T(8,128)(2,1)}, bf16[128,1024]{1,0:T(8,128)(2,1)}, u32[]{:S(2)}, u32[]{:S(2)}) collective-permute-start(bf16[128,1024]{1,0:T(8,128)(2,1)} %collective-permute-done.1), channel_id=1, source_target_pairs={{0,4},{1,5},{4,8},{5,9},{8,12},{9,13},{12,14},{13,15},{14,10},{15,... | collective-permute-start | bytes 786440 | tf_op jit(solution)/shard_map/ppermute | solution.py:223
  101.4 11.6 %collective-permute-start.4 = (bf16[128,1024]{1,0:T(8,128)(2,1)}, bf16[128,1024]{1,0:T(8,128)(2,1)}, u32[]{:S(2)}, u32[]{:S(2)}) collective-permute-start(bf16[128,1024]{1,0:T(8,128)(2,1)} %collective-permute-done.2), channel_id=1, source_target_pairs={{4,0},{5,1},{8,4},{9,5},{12,8},{13,9},{14,12},{15,13},{10,14},{11,... | collective-permute-start | bytes 786440 | tf_op jit(solution)/shard_map/ppermute | solution.py:224
  101.4 16.5 %all-to-all-start.2 = ((bf16[16,128,64]{1,2,0:T(8,128)(2,1)}), bf16[16,128,64]{1,2,0:T(8,128)(2,1)S(1)}, u32[]{:S(2)}, u32[]{:S(2)}) async-start(bf16[16,128,64]{1,2,0:T(8,128)(2,1)} %pad_maximum_fusion.3), calls=%async_computation.2 | async-start | bytes 524288 | tf_op jit(solution)/shard_map/all_to_all | solution.py:236
  108.8 5.6 %copy-start.14 = (bf16[192,1,128]{2,1,0:T(2,128)(2,1)S(1)}, bf16[192,1,128]{2,1,0:T(2,128)(2,1)}, u32[]{:S(2)}) copy-start(bf16[192,1,128]{2,1,0:T(2,128)(2,1)} %get-tuple-element.28) | copy-start | bytes 147460
  110.3 12.0 %collective-permute-start.5 = (bf16[128,1024]{1,0:T(8,128)(2,1)}, bf16[128,1024]{1,0:T(8,128)(2,1)}, u32[]{:S(2)}, u32[]{:S(2)}) collective-permute-start(bf16[128,1024]{1,0:T(8,128)(2,1)} %collective-permute-done.3), channel_id=1, source_target_pairs={{0,4},{1,5},{4,8},{5,9},{8,12},{9,13},{12,14},{13,15},{14,10},{15,... | collective-permute-start | bytes 786440 | tf_op jit(solution)/shard_map/ppermute | solution.py:223
  113.0 11.5 %collective-permute-start.6 = (bf16[128,1024]{1,0:T(8,128)(2,1)}, bf16[128,1024]{1,0:T(8,128)(2,1)}, u32[]{:S(2)}, u32[]{:S(2)}) collective-permute-start(bf16[128,1024]{1,0:T(8,128)(2,1)} %collective-permute-done.4), channel_id=1, source_target_pairs={{4,0},{5,1},{8,4},{9,5},{12,8},{13,9},{14,12},{15,13},{10,14},{11,... | collective-permute-start | bytes 786440 | tf_op jit(solution)/shard_map/ppermute | solution.py:224
  119.5 10.8 %copy-start.10 = (bf16[192,1,128]{2,1,0:T(2,128)(2,1)S(1)}, bf16[192,1,128]{2,1,0:T(2,128)(2,1)}, u32[]{:S(2)}) copy-start(bf16[192,1,128]{2,1,0:T(2,128)(2,1)} %get-tuple-element.24) | copy-start | bytes 147460
  119.5 11.0 %copy-start.2 = (f32[192,1024]{1,0:T(8,128)S(1)}, f32[192,1024]{1,0:T(8,128)}, u32[]{:S(2)}) copy-start(f32[192,1024]{1,0:T(8,128)} %fusion.3) | copy-start | bytes 2359300
  119.5 11.0 %copy-start.13 = (bf16[192,1,128]{2,1,0:T(2,128)(2,1)S(1)}, bf16[192,1,128]{2,1,0:T(2,128)(2,1)}, u32[]{:S(2)}) copy-start(bf16[192,1,128]{2,1,0:T(2,128)(2,1)} %get-tuple-element.23) | copy-start | bytes 147460
  123.3 4.1 %collective-permute-start.7 = (bf16[64,1024]{1,0:T(8,128)(2,1)S(1)}, bf16[64,1024]{1,0:T(8,128)(2,1)S(1)}, u32[]{:S(2)}, u32[]{:S(2)}) collective-permute-start(bf16[64,1024]{1,0:T(8,128)(2,1)S(1)} %slice.72), channel_id=1, source_target_pairs={{0,4},{1,5},{4,8},{5,9},{8,12},{9,13},{12,14},{13,15},{14,10},{15,... | collective-permute-start | bytes 393224 | tf_op jit(solution)/shard_map/ppermute | solution.py:230
  125.4 4.9 %collective-permute-start.8 = (bf16[64,1024]{1,0:T(8,128)(2,1)S(1)}, bf16[64,1024]{1,0:T(8,128)(2,1)S(1)}, u32[]{:S(2)}, u32[]{:S(2)}) collective-permute-start(bf16[64,1024]{1,0:T(8,128)(2,1)S(1)} %slice.73), channel_id=1, source_target_pairs={{4,0},{5,1},{8,4},{9,5},{12,8},{13,9},{14,12},{15,13},{10,14},{11,... | collective-permute-start | bytes 393224 | tf_op jit(solution)/shard_map/ppermute | solution.py:231
  130.5 4.1 %copy-start.9 = (bf16[16,16,2,64]{3,2,1,0:T(2,128)(2,1)S(1)}, bf16[16,16,2,64]{3,2,1,0:T(2,128)(2,1)}, u32[]{:S(2)}) copy-start(bf16[16,16,2,64]{3,2,1,0:T(2,128)(2,1)} %copy.82) | copy-start | bytes 196612
  133.5 6.6 %collective-permute-start.9 = (f32[96,1024]{1,0:T(8,128)}, f32[96,1024]{1,0:T(8,128)}, u32[]{:S(2)}, u32[]{:S(2)}) collective-permute-start(f32[96,1024]{1,0:T(8,128)} %slice.75), channel_id=1, source_target_pairs={{0,1},{1,0},{2,3},{3,2},{4,5},{5,4},{6,7},{7,6},{8,9},{9,8},{10,11... | collective-permute-start | bytes 1179656 | tf_op jit(solution)/shard_map/ppermute | solution.py:233
  134.6 5.5 %copy-start.4 = (f32[192,1024]{1,0:T(8,128)S(1)}, f32[192,1024]{1,0:T(8,128)}, u32[]{:S(2)}) copy-start(f32[192,1024]{1,0:T(8,128)} %copy-done.3) | copy-start | bytes 2359300
  (1 other events, 0.9 us)
Sparse Core Ops, SparseCore 0:
  10.2 45.6 all-gather.2
  58.0 38.2 all-gather.4
